TPU v7x, 32 devices: a whole 2x2x4 slice. The times are simulated.
32 devices in a mesh: tile: 8 (over z, x), lev: 4 (over y, core).
Axes of the slice: x: 2, y: 2, z: 4, core: 2. Of those that a mesh axis runs over, the one named last changes fastest.
Arguments:
- krylov: bfloat16 [4, 8, 5, 2048, 128], P(None, 'lev', None, 'tile'), may hold values from -7 to 7, as said below
- adjoint: float32 [8, 5, 2048, 128], P('lev', None, 'tile'), may hold values from -200 to 200
- projected: float32 [4, 4], replicated, may hold values from -3 to 3
- stencil: bfloat16 [5, 8, 2048, 128], P(None, 'lev', 'tile'), may hold values from 0.19921875 to 1
- column_weight: float32 [2, 8, 2048, 128], P(None, 'lev', 'tile'), may hold values from 0.05 to 0.3
- seam_turns: int32 [8, 4], P('tile'), may hold values from 0 to 3
Outputs:
- updated: float32 [8, 5, 2048, 128], P('lev', None, 'tile')
Inputs may be any that keep to these rules, and one draw needn't show every extreme that they name: `krylov`: krylov vectors of order one.
All inputs are finite; a program needn't handle non-finite values.
Results may differ from a plain program's by a relative error of at most 0.0003.
Values sent between devices are 32-bit elements; how exact they have to be, the bound alone decides.
No kernel may reach another device: no remote copies, remote signals or barrier semaphores. Data moves between devices by JAX's collectives and lax.ppermute only.
A program may use at most 128 MiB of HBM per device.

v0:
```python
import jax
import jax.numpy as jnp
from jax import lax
from jax.sharding import PartitionSpec as P

STRIDE = 4


def entering(x, axis, combine, identity):
    peers, here = (lax.axis_size(axis), lax.axis_index(axis))
    everything = lax.all_gather(x, axis)
    start = jnp.broadcast_to(jnp.asarray(identity, x.dtype), x.shape)

    def step(k, before):
        at = peers - 1 - k
        reached = at > here
        new = combine(before, everything[at])
        return jnp.where(reached, new, before)

    return lax.fori_loop(0, peers, step, start)


def with_halo(block, sides, width):
    for axis, dim in sides:
        count = lax.axis_size(axis)
        forward = [(i, i + 1) for i in range(count - 1)]
        forward.append((count - 1, 0))
        backward = [(target, source) for source, target in forward]
        low = lax.ppermute(
            lax.slice_in_dim(block, block.shape[dim] - width, None, axis=dim), axis, forward
        )
        high = lax.ppermute(lax.slice_in_dim(block, 0, width, axis=dim), axis, backward)
        block = jnp.concatenate([low, block, high], axis=dim)
    return block


def shifted(value, axis, steps):
    count = lax.axis_size(axis)
    pairs = [(source, (source + steps) % count) for source in range(count)]
    return lax.ppermute(value, axis, pairs)


def rotate(edge_strip, turning):
    flipped = jnp.where(turning % 2 == 1, edge_strip[..., ::-1], edge_strip)
    cosine = jnp.where(turning == 0, 1.0, jnp.where(turning == 2, -1.0, 0.0)).astype(
        edge_strip.dtype
    )
    sine_part = jnp.where(turning == 1, 1.0, jnp.where(turning == 3, -1.0, 0.0)).astype(
        edge_strip.dtype
    )
    wind_east = flipped[..., 2:3, :]
    wind_north = flipped[..., 3:4, :]
    turned_u = cosine * wind_east - sine_part * wind_north
    turned_v = sine_part * wind_east + cosine * wind_north
    return jnp.concatenate([flipped[..., :2, :], turned_u, turned_v, flipped[..., 4:, :]], axis=-2)


def add_pair(earlier, later):
    return earlier + later


def column_totals_below(totals):
    return entering(totals, "lev", add_pair, jnp.zeros_like(totals))


def apply_operator(field, stencil, column_weight, seam_turns):
    coeffs = stencil.astype(jnp.float32)[:, None, :, None]
    image = coeffs[0] * field
    plus_rows = coeffs[1] * field
    minus_rows = coeffs[2] * field
    edge_pairs = jnp.stack([minus_rows[..., 0, :], plus_rows[..., -1, :]], axis=0)
    padded = with_halo(edge_pairs, (("tile", 0),), 1)
    from_lower = rotate(padded[0], seam_turns[0, 0])
    from_upper = rotate(padded[3], seam_turns[0, 1])
    image = image + jnp.concatenate([from_lower[..., None, :], plus_rows[..., :-1, :]], axis=-2)
    image = image + jnp.concatenate([minus_rows[..., 1:, :], from_upper[..., None, :]], axis=-2)
    plus_cols = coeffs[3] * field
    minus_cols = coeffs[4] * field
    up_strip = shifted(plus_cols[..., -1], "tile", STRIDE)
    down_strip = shifted(minus_cols[..., 0], "tile", -STRIDE)
    up_strip = rotate(up_strip, seam_turns[0, 2])
    down_strip = rotate(down_strip, seam_turns[0, 3])
    image = image + jnp.concatenate([up_strip[..., None], plus_cols[..., :-1]], axis=-1)
    image = image + jnp.concatenate([minus_cols[..., 1:], down_strip[..., None]], axis=-1)
    carried = jnp.stack([field[:, :, 0], field[:, :, 3]], axis=2)
    totals = jnp.sum(carried, axis=1)
    below = column_totals_below(totals)
    suffix = jnp.cumsum(carried[:, ::-1], axis=1)[:, ::-1] + below[:, None]
    weights = jnp.moveaxis(column_weight, 0, 1)[None]
    scaled = suffix * weights
    zeros_part = jnp.zeros_like(scaled[:, :, 0])
    column_part = jnp.stack(
        [zeros_part, scaled[:, :, 0], zeros_part, zeros_part, scaled[:, :, 1]], axis=2
    )
    return image + column_part


def per_device(krylov, adjoint, projected, stencil, column_weight, seam_turns):
    vectors = krylov.astype(jnp.float32)
    partial_value = jnp.sum(vectors * adjoint[None], axis=(1, 2, 3, 4))
    count = (
        adjoint.shape[0]
        * adjoint.shape[1]
        * adjoint.shape[2]
        * adjoint.shape[3]
        * lax.axis_size("tile")
        * lax.axis_size("lev")
    )
    coupling = lax.psum(partial_value, ("tile", "lev")) / count
    mixing = jnp.sum(projected * coupling[:, None], axis=0)
    images = apply_operator(vectors, stencil, column_weight, seam_turns)
    total_image = jnp.sum(mixing[:, None, None, None, None] * images, axis=0)
    return adjoint + 0.5 * total_image


def solution(mesh):
    placed = (
        P(None, "lev", None, "tile", None),
        P("lev", None, "tile", None),
        P(),
        P(None, "lev", "tile", None),
        P(None, "lev", "tile", None),
        P("tile", None),
    )
    return jax.shard_map(
        per_device,
        mesh=mesh,
        in_specs=placed,
        out_specs=P("lev", None, "tile", None),
        check_vma=False,
    )
```

profile of v0, /device:TPU:0, one launch (start us, length us, event | category | flops | bytes accessed | tf_op | source)
XLA Modules:
  0.0 157.3 jit_solution(6583245279324220647)
XLA Ops:
  6.5 1.5 fusion.9
  8.0 0.0 copy-start.1
  8.0 2.6 %fusion.8 = (f32[4,2,256,128]{3,2,1,0:T(8,128)}, f32[4,2,2,256,128]{4,3,2,1,0:T(8,128)}) fusion(f32[4,2,1,256,128]{4,3,2,1,0:T(8,128)S(1)} %get-tuple-element.145, f32[4,2,1,256,128]{4,3,2,1,0:T(8,128)S(1)} %get-tuple-element.144), kind=kLoop, calls=%fused_computation.45 | loop fusion | flops 786432 | bytes 5242880 | tf_op jit(solution)/shard_map/reduce_sum | solution.py:86
  10.7 0.0 all-gather.3.cloned.1.call-update
  10.7 1.2 convert_element_type.7
  11.9 1.0 slice_bitcast_fusion.4
  12.9 11.2 %fusion = (f32[4]{0:T(128)S(1)}, f32[4,2,5,256,128]{4,3,2,1,0:T(8,128)}, f32[4,2,5,256,128]{4,3,2,1,0:T(8,128)}, f32[4,2,5,256,128]{4,3,2,1,0:T(8,128)}, f32[4,2,5,256,128]{4,3,2,1,0:T(8,128)}) fusion(bf16[4,2,5,256,128]{4,3,2,1,0:T(8,128)(2,1)S(1)} %copy-done.1, f32[2,5,256,128]{3,2,1,0:T(8,128)} %param.9, f32[2,256,128]{2,1,0:T(8,128)} %get-tuple-element.154, ...), kind=kLoop, calls=%fused_computation.7 | loop fusion | flops 9175036 | bytes 25952272 | tf_op jit(solution)/shard_map/reduce_sum | solution.py:100
  24.1 0.9 slice_bitcast_fusion.5
  25.0 5.8 %collective-permute-start.1 = (f32[1,4,2,5,128]{4,0,3,2,1:T(1,128)S(1)}, f32[1,4,2,5,128]{4,0,3,2,1:T(1,128)S(1)}, u32[]{:S(2)}, u32[]{:S(2)}) collective-permute-start(f32[1,4,2,5,128]{4,0,3,2,1:T(1,128)S(1)} %slice_bitcast_fusion.5), channel_id=1, source_target_pairs={{4,0},{8,4},{12,8},{16,12},{20,16},{24,20},{28,24},{0,28},{5,1},{9... | collective-permute-start | bytes 61448 | tf_op jit(solution)/shard_map/ppermute | solution.py:32
  30.8 0.9 slice_bitcast_fusion.6
  31.8 0.1 collective-permute-start
  31.8 3.3 %copy.38 = f32[4,2,5,256,1]{3,1,2,0,4:T(2,128)S(1)} copy(f32[4,2,5,256,1]{4,3,2,1,0:T(8,128)} %bitcast.52) | data formatting | bytes 81920 | tf_op jit(solution)/shard_map/slice | solution.py:80
  35.2 0.1 collective-permute-start.3
  35.3 6.3 %slice.169 = f32[4,2,5,256,1]{4,3,2,1,0:T(8,128)} slice(f32[4,2,5,256,128]{4,3,2,1,0:T(8,128)} %get-tuple-element.142), slice={[0:4], [0:2], [0:5], [0:256], [127:128]} | slice | bytes 81920 | tf_op jit(solution)/shard_map/slice | solution.py:79
  41.6 3.4 %copy.36 = f32[4,2,5,256,1]{3,1,2,0,4:T(2,128)S(1)} copy(f32[4,2,5,256,1]{4,3,2,1,0:T(8,128)} %slice.169) | data formatting | bytes 81920 | tf_op jit(solution)/shard_map/slice | solution.py:79
  45.1 2.9 %collective-permute-start.2 = (f32[4,2,5,256]{3,1,2,0:T(2,128)S(1)}, f32[4,2,5,256]{3,1,2,0:T(2,128)S(1)}, u32[]{:S(2)}, u32[]{:S(2)}) collective-permute-start(f32[4,2,5,256]{3,1,2,0:T(2,128)S(1)} %bitcast.62), channel_id=1, source_target_pairs={{0,16},{4,20},{8,24},{12,28},{16,0},{20,4},{24,8},{28,12},{1,17},{... | collective-permute-start | bytes 122888 | tf_op jit(solution)/shard_map/ppermute | solution.py:40
  48.0 40.3 %psum.7 = f32[4]{0:T(128)S(1)} all-reduce(f32[4]{0:T(128)S(1)} %get-tuple-element.139), channel_id=1, replica_groups=mesh['tile'=8,'lev'=4] {'tile','lev'}, use_global_device_ids=true, to_apply=%region_1.0 | all-reduce | flops 4 | bytes 32 | tf_op jit(solution)/shard_map/psum | solution.py:109
  88.2 1.5 rev.22
  89.7 0.1 multiply_reduce_fusion
  89.8 3.2 %fusion.12 = f32[4,2,2,256,128]{4,3,2,1,0:T(8,128)} fusion(f32[4,2,2,256,128]{4,3,2,1,0:T(8,128)} %rev.22), kind=kOutput, calls=%fused_computation.49 | output fusion | flops 524288 | bytes 4194304 | tf_op jit(solution)/shard_map/jit(cumsum)/reduce_window_sum | solution.py:88
  93.1 0.7 fusion.11
  111.3 0.0 slice-start.1
  111.4 5.5 %slice.162 = f32[4,2,5,255,128]{4,3,2,1,0:T(8,128)} slice(f32[4,2,5,256,128]{4,3,2,1,0:T(8,128)} %get-tuple-element.141), slice={[0:4], [0:2], [0:5], [1:256], [0:128]} | slice | bytes 10444800 | tf_op jit(solution)/shard_map/slice | solution.py:76
  116.9 3.8 %slice.176 = f32[4,2,5,256,127]{4,3,2,1,0:T(8,128)} slice(f32[4,2,5,256,128]{4,3,2,1,0:T(8,128)S(1)} %bitcast.54), slice={[0:4], [0:2], [0:5], [0:256], [1:128]} | slice | bytes 10403840 | tf_op jit(solution)/shard_map/slice | solution.py:84
  120.7 0.1 pad.2.clone
  120.8 0.0 collective-permute-done.1
  120.9 0.1 rev.19
  121.0 0.0 collective-permute-done
  121.1 0.1 rev.18
  121.3 0.0 collective-permute-done.3
  121.4 0.3 rev.21
  121.7 3.2 %copy.39 = f32[4,2,5,256,1]{4,3,2,1,0:T(8,128)} copy(f32[4,2,5,256,1]{3,1,2,0,4:T(2,128)S(1)} %maximum_bitcast_fusion.1) | data formatting | bytes 81920 | tf_op jit(solution)/shard_map/broadcast_in_dim | solution.py:84
  124.9 0.3 rev.20
  125.3 3.1 %copy.37 = f32[4,2,5,256,1]{4,3,2,1,0:T(8,128)} copy(f32[4,2,5,256,1]{3,1,2,0,4:T(2,128)S(1)} %maximum_bitcast_fusion) | data formatting | bytes 81920 | tf_op jit(solution)/shard_map/broadcast_in_dim | solution.py:83
  128.4 6.4 %while.16 = (s32[]{:T(128)}, f32[4,2,256,128]{3,2,1,0:T(8,128)S(1)}, s32[]{:T(128)}, f32[4,4,2,256,128]{4,3,2,1,0:T(8,128)}, s32[]{:T(128)}, /*index=5*/s32[]{:T(128)}, s32[]{:T(128)}, s32[]{:T(128)}) while((s32[]{:T(128)}, f32[4,2,256,128]{3,2,1,0:T(8,128)S(1)}, s32[]{:T(128)}, f32[4,4,2,256,128]{4,3,2,1,0:T(8,128)}, s32[]{:T(128)}, ...), condition=%wide.region_6.7_spmd.clone, body=%wide.region_5.6_spmd.clone.sunk | while | flops 786440 | bytes 3145891 | solution.py:20
  128.4 1.6 %add_select_fusion.2 = f32[4,2,256,128]{3,2,1,0:T(8,128)S(1)} fusion(f32[4,2,256,128]{3,2,1,0:T(8,128)S(1)} %get-tuple-element.205, f32[4,4,2,256,128]{4,3,2,1,0:T(8,128)} %get-tuple-element.215, s32[]{:T(128)S(6)} %select_n.175, pred[]{:T(512)S(6)} %compare.7, pred[]{:T(512)S(6)} %gt.12), kind=kLoop, calls=%fused_computation.clone.1 | loop fusion | flops 786432 | bytes 3145734 | tf_op jit(solution)/shard_map/while/body/eval_jaxpr/jit(_where)/select_n | solution.py:18
  130.0 1.6 %add_select_fusion.2 = f32[4,2,256,128]{3,2,1,0:T(8,128)S(1)} fusion(f32[4,2,256,128]{3,2,1,0:T(8,128)S(1)} %get-tuple-element.205, f32[4,4,2,256,128]{4,3,2,1,0:T(8,128)} %get-tuple-element.215, s32[]{:T(128)S(6)} %select_n.175, pred[]{:T(512)S(6)} %compare.7, pred[]{:T(512)S(6)} %gt.12), kind=kLoop, calls=%fused_computation.clone.1 | loop fusion | flops 786432 | bytes 3145734 | tf_op jit(solution)/shard_map/while/body/eval_jaxpr/jit(_where)/select_n | solution.py:18
  131.6 1.6 %add_select_fusion.2 = f32[4,2,256,128]{3,2,1,0:T(8,128)S(1)} fusion(f32[4,2,256,128]{3,2,1,0:T(8,128)S(1)} %get-tuple-element.205, f32[4,4,2,256,128]{4,3,2,1,0:T(8,128)} %get-tuple-element.215, s32[]{:T(128)S(6)} %select_n.175, pred[]{:T(512)S(6)} %compare.7, pred[]{:T(512)S(6)} %gt.12), kind=kLoop, calls=%fused_computation.clone.1 | loop fusion | flops 786432 | bytes 3145734 | tf_op jit(solution)/shard_map/while/body/eval_jaxpr/jit(_where)/select_n | solution.py:18
  133.2 1.6 %add_select_fusion.2 = f32[4,2,256,128]{3,2,1,0:T(8,128)S(1)} fusion(f32[4,2,256,128]{3,2,1,0:T(8,128)S(1)} %get-tuple-element.205, f32[4,4,2,256,128]{4,3,2,1,0:T(8,128)} %get-tuple-element.215, s32[]{:T(128)S(6)} %select_n.175, pred[]{:T(512)S(6)} %compare.7, pred[]{:T(512)S(6)} %gt.12), kind=kLoop, calls=%fused_computation.clone.1 | loop fusion | flops 786432 | bytes 3145734 | tf_op jit(solution)/shard_map/while/body/eval_jaxpr/jit(_where)/select_n | solution.py:18
  134.9 0.0 copy-start.2
  134.9 0.0 slice-start.3
  134.9 1.9 %add_multiply_fusion = f32[4,2,2,256,128]{4,3,2,1,0:T(8,128)S(1)} fusion(f32[4,2,2,256,128]{4,3,2,1,0:T(8,128)} %fusion.12, f32[4,2,256,128]{3,2,1,0:T(8,128)S(1)} %get-tuple-element.115, f32[2,2,256,128]{3,2,1,0:T(8,128)S(1)} %copy-done), kind=kLoop, calls=%fused_computation.16 | loop fusion | flops 1048576 | bytes 5767168 | tf_op jit(solution)/shard_map/mul | solution.py:90
  136.8 0.2 fusion.10
  137.0 0.6 slice-done.2
  137.7 0.8 copy-done.2
  138.5 0.2 slice-done.3
  138.7 10.5 %fusion.7 = f32[2,5,256,128]{3,2,1,0:T(8,128)S(1)} fusion(bf16[4,2,5,256,128]{4,3,2,1,0:T(8,128)(2,1)S(1)} %copy-done.2, f32[4,2,5,255,128]{4,3,2,1,0:T(8,128)} %bitcast.58, f32[4,2,5,1,128]{4,3,2,1,0:T(1,128)S(1)} %copy.33, f32[4,2,5,1,128]{4,3,2,1,0:T(1,128)S(1)} %copy.35, f32[4,2,5,255,128]{4,3,2,1,0:T(8,128)} %slice.162, ...), kind=kLoop, calls=%fused_computation.14 | loop fusion | flops 20643840 | bytes 27263032 | tf_op jit(solution)/shard_map/reduce_sum | solution.py:112
  149.3 1.2 multiply_add_fusion
  (44 shorter events, 0.3 us)
Async XLA Ops:
  6.5 128.3 %copy-start = (f32[2,2,256,128]{3,2,1,0:T(8,128)S(1)}, f32[2,2,256,128]{3,2,1,0:T(8,128)}, u32[]{:S(2)}) copy-start(f32[2,2,256,128]{3,2,1,0:T(8,128)} %param.12) | copy-start | bytes 1572868
  6.5 121.9 %all-gather.3.cloned.1.call-start = ((), (), s32[]{:S(2)}) async-start(), calls=%async_computation | async-start | bytes 5242880 | tf_op jit(solution)/shard_map/all_gather | solution.py:11
  8.0 4.9 %copy-start.1 = (bf16[4,2,5,256,128]{4,3,2,1,0:T(8,128)(2,1)S(1)}, bf16[4,2,5,256,128]{4,3,2,1,0:T(8,128)(2,1)}, u32[]{:S(2)}) copy-start(bf16[4,2,5,256,128]{4,3,2,1,0:T(8,128)(2,1)} %param.8) | copy-start | bytes 7864324
  25.0 95.8 %collective-permute-start.1 = (f32[1,4,2,5,128]{4,0,3,2,1:T(1,128)S(1)}, f32[1,4,2,5,128]{4,0,3,2,1:T(1,128)S(1)}, u32[]{:S(2)}, u32[]{:S(2)}) collective-permute-start(f32[1,4,2,5,128]{4,0,3,2,1:T(1,128)S(1)} %slice_bitcast_fusion.5), channel_id=1, source_target_pairs={{4,0},{8,4},{12,8},{16,12},{20,16},{24,20},{28,24},{0,28},{5,1},{9... | collective-permute-start | bytes 61448 | tf_op jit(solution)/shard_map/ppermute | solution.py:32
  31.8 89.2 %collective-permute-start = (f32[1,4,2,5,128]{4,0,3,2,1:T(1,128)S(1)}, f32[1,4,2,5,128]{4,0,3,2,1:T(1,128)S(1)}, u32[]{:S(2)}, u32[]{:S(2)}) collective-permute-start(f32[1,4,2,5,128]{4,0,3,2,1:T(1,128)S(1)} %slice_bitcast_fusion.6), channel_id=1, source_target_pairs={{0,4},{4,8},{8,12},{12,16},{16,20},{20,24},{24,28},{28,0},{1,5},{5... | collective-permute-start | bytes 61448 | tf_op jit(solution)/shard_map/ppermute | solution.py:29
  35.2 86.2 %collective-permute-start.3 = (f32[4,2,5,256]{3,1,2,0:T(2,128)S(1)}, f32[4,2,5,256]{3,1,2,0:T(2,128)S(1)}, u32[]{:S(2)}, u32[]{:S(2)}) collective-permute-start(f32[4,2,5,256]{3,1,2,0:T(2,128)S(1)} %bitcast.63), channel_id=1, source_target_pairs={{0,16},{4,20},{8,24},{12,28},{16,0},{20,4},{24,8},{28,12},{1,17},{... | collective-permute-start | bytes 122888 | tf_op jit(solution)/shard_map/ppermute | solution.py:40
  41.6 46.6 %copy-start.3 = (f32[4,2,2,256,128]{4,3,2,1,0:T(8,128)S(1)}, f32[4,2,2,256,128]{4,3,2,1,0:T(8,128)}, u32[]{:S(2)}) copy-start(f32[4,2,2,256,128]{4,3,2,1,0:T(8,128)} %get-tuple-element.149) | copy-start | bytes 6291460
  41.6 48.1 %copy-start.6 = (f32[4,4]{1,0:T(4,128)S(1)}, f32[4,4]{1,0:T(4,128)}, u32[]{:S(2)}) copy-start(f32[4,4]{1,0:T(4,128)} %param.10) | copy-start | bytes 196
  45.1 48.0 %copy-start.5 = (s32[1,4]{1,0:T(1,128)S(1)}, s32[1,4]{1,0:T(1,128)}, u32[]{:S(2)}) copy-start(s32[1,4]{1,0:T(1,128)} %param.13) | copy-start | bytes 52
  45.1 79.9 %collective-permute-start.2 = (f32[4,2,5,256]{3,1,2,0:T(2,128)S(1)}, f32[4,2,5,256]{3,1,2,0:T(2,128)S(1)}, u32[]{:S(2)}, u32[]{:S(2)}) collective-permute-start(f32[4,2,5,256]{3,1,2,0:T(2,128)S(1)} %bitcast.62), channel_id=1, source_target_pairs={{0,16},{4,20},{8,24},{12,28},{16,0},{20,4},{24,8},{28,12},{1,17},{... | collective-permute-start | bytes 122888 | tf_op jit(solution)/shard_map/ppermute | solution.py:40
  89.8 27.1 %slice-start = ((s8[5242880]{0:T(1024)(128)(4,1)}), s8[1048576]{0:T(1024)(128)(4,1)S(1)}, s32[]{:S(2)}) async-start(s8[5242880]{0:T(1024)(128)(4,1)} %bitcast.53), calls=%async_computation.1 | async-start | bytes 2097152
  111.3 5.6 %slice-start.1 = ((s8[5242880]{0:T(1024)(128)(4,1)}), s8[4194304]{0:T(1024)(128)(4,1)S(1)}, s32[]{:S(2)}) async-start(s8[5242880]{0:T(1024)(128)(4,1)} %bitcast.53), calls=%async_computation.2 | async-start | bytes 8388608
  134.8 2.8 %slice-start.2 = ((s8[5242880]{0:T(1024)(128)(4,1)}), s8[4194304]{0:T(1024)(128)(4,1)S(1)}, s32[]{:S(2)}) async-start(s8[5242880]{0:T(1024)(128)(4,1)} %bitcast.55), calls=%async_computation.3 | async-start | bytes 8388608
  134.9 3.6 %copy-start.2 = (bf16[4,2,5,256,128]{4,3,2,1,0:T(8,128)(2,1)S(1)}, bf16[4,2,5,256,128]{4,3,2,1,0:T(8,128)(2,1)}, u32[]{:S(2)}) copy-start(bf16[4,2,5,256,128]{4,3,2,1,0:T(8,128)(2,1)} %param.8) | copy-start | bytes 7864324
  134.9 3.8 %slice-start.3 = ((s8[5242880]{0:T(1024)(128)(4,1)}), s8[1048576]{0:T(1024)(128)(4,1)S(1)}, s32[]{:S(2)}) async-start(s8[5242880]{0:T(1024)(128)(4,1)} %bitcast.55), calls=%async_computation.4 | async-start | bytes 2097152
  138.7 10.5 %copy-start.4 = (f32[2,5,256,128]{3,2,1,0:T(8,128)S(1)}, f32[2,5,256,128]{3,2,1,0:T(8,128)}, u32[]{:S(2)}) copy-start(f32[2,5,256,128]{3,2,1,0:T(8,128)} %param.9) | copy-start | bytes 3932164
Sparse Core Ops, SparseCore 0:
  10.8 37.1 all-gather.2
where the time goes:
time: 158 us; the launch traced here: 157 us
  blocking collectives  40.3 us (26%)
  other arithmetic  38.6 us (24%)
  local copies, waits for them, and re-layouts  38 us (24%)
  between operations  31.4 us (20%)
  starting transfers between devices  8.9 us (6%)
    psum x1, blocking collectives, per_device(): coupling = lax.psum(partial_value, ('tile', 'lev')) / count  40.3 us
    reduce_sum x1, other arithmetic, per_device(): partial_value = jnp.sum(vectors * adjoint[None], axis=(1, 2, 3, 4))  11.2 us
    reduce_sum x1, other arithmetic, per_device(): total_image = jnp.sum(mixing[:, None, None, None, None] * images, axis=0)  10.5 us
    slice x2, local copies, waits for them, and re-layouts, apply_operator(): up_strip = shifted(plus_cols[..., -1], 'tile', STRIDE)  9.72 us
    select_n x4, other arithmetic, step(): return jnp.where(reached, new, before)  6.34 us
    ppermute x1, starting transfers between devices, with_halo(): lax.ppermute(lax.slice_in_dim(block, 0, width, axis=dim), axis, backward)  5.79 us
    slice x1, local copies, waits for them, and re-layouts, apply_operator(): minus_rows[..., 1:, :]  5.55 us
    slice x1, local copies, waits for them, and re-layouts, apply_operator(): minus_cols[..., 1:]  3.78 us
  transfers between devices with their start and end apart: 5, of which 0 were waited for; matrix products, arithmetic and copies ran while one was open for 32% of the time, Pallas kernels for 0%

commit v1 on v0

v1 whole, which is shorter than its diff:
```python
import functools

import jax
import jax.numpy as jnp
from jax import lax
from jax.experimental import pallas as pl
from jax.experimental.pallas import tpu as pltpu
from jax.sharding import PartitionSpec as P

STRIDE = 4
F32 = jnp.float32
VMEM_LIMIT = 24 * 1024 * 1024

ANY = pl.BlockSpec(memory_space=pl.ANY)
IN_VMEM = pl.BlockSpec(memory_space=pltpu.VMEM)
IN_SMEM = pl.BlockSpec(memory_space=pltpu.SMEM)


def pinned(x):
    return pltpu.with_memory_space_constraint(x, pltpu.VMEM)


def exchange(x, axis, bit):
    size = lax.axis_size(axis)
    return lax.ppermute(x, axis, [(i, i ^ bit) for i in range(size)])


def shifted(x, axis, steps):
    size = lax.axis_size(axis)
    return lax.ppermute(x, axis, [(i, (i + steps) % size) for i in range(size)])


def bits(axis):
    size = lax.axis_size(axis)
    return [1 << b for b in range(size.bit_length() - 1)]


def lanes(shape):
    return lax.broadcasted_iota(jnp.int32, shape, len(shape) - 1)


def rows(shape):
    return lax.broadcasted_iota(jnp.int32, shape, len(shape) - 2)


def dots_kernel(dims, core, kry, adj, kry_v, adj_v, part, mine, theirs, sums, sem_k, sem_a):
    vectors, levels, fields, height = dims
    half = vectors // 2
    order = [0, 3] + [f for f in range(fields) if f not in (0, 3)]
    copies = []
    for f in order:
        for l in range(levels):
            n = f * levels + l
            copies.append(
                (
                    f,
                    l,
                    pltpu.make_async_copy(kry.at[:, l, f], kry_v.at[:, l, f], sem_k.at[n]),
                    pltpu.make_async_copy(adj.at[l, f], adj_v.at[l, f], sem_a.at[n]),
                )
            )
    for _, _, a, b in copies:
        a.start()
        b.start()
    step = 32
    accs = [jnp.zeros((8, 128), F32) for _ in range(vectors)]
    for f, l, a, b in copies:
        a.wait()
        b.wait()

        def body(i, accs, f=f, l=l):
            at = pl.ds(pl.multiple_of(i * step, step), step)
            y = adj_v[l, f, at]
            out = []
            for k in range(vectors):
                x = kry_v[k, l, f, at].astype(F32)
                if f in (0, 3):
                    c = 0 if f == 0 else 1
                    if l == 0:
                        sums[k, c, at] = x
                    else:
                        sums[k, c, at] = sums[k, c, at] + x
                p = x * y
                out.append(accs[k] + jnp.sum(p.reshape(step // 8, 8, 128), axis=0))
            return out

        accs = lax.fori_loop(0, height // step, body, accs)
    low = core[0] == 0
    for k in range(half):

        @pl.when(low)
        def _(k=k):
            mine[k] = sums[k]
            theirs[k] = sums[half + k]

        @pl.when(jnp.logical_not(low))
        def _(k=k):
            mine[k] = sums[half + k]
            theirs[k] = sums[k]

    total = jnp.zeros((8, 128), F32)
    r = rows((8, 128))
    for k in range(vectors):
        total = jnp.where(r == k, jnp.sum(accs[k], axis=0, keepdims=True), total)
    part[...] = total


def strips_kernel(dims, kry_v, sten, cw, sten_v, cw_v, fwd, back, cols, sem):
    vectors, levels, fields, height = dims
    c1 = pltpu.make_async_copy(sten, sten_v, sem.at[0])
    c2 = pltpu.make_async_copy(cw, cw_v, sem.at[1])
    c1.start()
    c2.start()
    c1.wait()
    per = levels * fields
    fwd[...] = jnp.zeros_like(fwd)
    back[...] = jnp.zeros_like(back)
    tail = height - 16
    for l in range(levels):
        last = sten_v[1, l, tail:height].astype(F32)[15:16]
        first = sten_v[2, l, 0:16].astype(F32)[0:1]
        for k in range(vectors):
            for f in range(fields):
                s = k * 16 + l * fields + f
                fwd[s : s + 1] = kry_v[k, l, f, tail:height].astype(F32)[15:16] * last
                back[s : s + 1] = kry_v[k, l, f, 0:16].astype(F32)[0:1] * first
    step = 32

    def body(i, carry):
        at = pl.ds(pl.multiple_of(i * step, step), step)
        lane = lanes((step, 128))
        x = jnp.zeros((step, 128), F32)
        coeff = jnp.zeros((step, 128), F32)
        for l in range(levels):
            up = jnp.broadcast_to(sten_v[3, l, at].astype(F32)[:, 127:128], (step, 128))
            down = jnp.broadcast_to(sten_v[4, l, at].astype(F32)[:, 0:1], (step, 128))
            both = jnp.where(lane % 2 == 0, up, down)
            coeff = jnp.where(lane % (2 * per) // (2 * fields) == l, both, coeff)
            for k in range(vectors):
                for f in range(fields):
                    s = k * per + l * fields + f
                    moved = pltpu.roll(kry_v[k, l, f, at].astype(F32), 2 * s + 1, 1)
                    x = jnp.where(lane // 2 == s, moved, x)
        cols[at] = x * coeff
        return carry

    lax.fori_loop(0, height // step, body, 0)
    c2.wait()


def turn_of(r):
    cosine = jnp.where(r == 0, 1.0, jnp.where(r == 2, -1.0, 0.0)).astype(F32)
    sine = jnp.where(r == 1, 1.0, jnp.where(r == 3, -1.0, 0.0)).astype(F32)
    return cosine, sine


def turn_kernel(dims, turns, fwd, back, up, down, fwd_o, back_o, cols_o):
    vectors, levels, fields, height = dims
    per = levels * fields
    n = vectors * 16
    flip = (lanes((128, 128)) + rows((128, 128)) == 127).astype(F32)
    r = rows((n, 128)) % 16
    field = r % fields
    real = r < per
    for side, strip, out in ((0, fwd, fwd_o), (1, back, back_o)):
        turning = turns[0, side]
        x = strip[...]
        x = jnp.where(
            turning % 2 == 1,
            jnp.dot(x, flip, precision=lax.Precision.HIGHEST, preferred_element_type=F32),
            x,
        )
        cosine, sine = turn_of(turning)
        u = cosine * x - sine * pltpu.roll(x, n - 1, 0)
        v = sine * pltpu.roll(x, 1, 0) + cosine * x
        out[...] = jnp.where(real & (field == 2), u, jnp.where(real & (field == 3), v, x))
    lane = lanes((height, 128))
    even = lane % 2 == 0
    x = jnp.where(even, up[...], down[...])
    mirror = (lanes((height, height)) + rows((height, height)) == height - 1).astype(F32)
    mirrored = jnp.dot(mirror, x, precision=lax.Precision.HIGHEST, preferred_element_type=F32)
    t_up, t_down = turns[0, 2], turns[0, 3]
    odd = jnp.where(even, t_up % 2, t_down % 2)
    x = jnp.where(odd == 1, mirrored, x)
    cos_u, sin_u = turn_of(t_up)
    cos_d, sin_d = turn_of(t_down)
    cosine = jnp.where(even, cos_u, cos_d)
    sine = jnp.where(even, sin_u, sin_d)
    field = lane % (2 * fields) // 2
    u = cosine * x - sine * pltpu.roll(x, 126, 1)
    v = sine * pltpu.roll(x, 2, 1) + cosine * x
    x = jnp.where(field == 2, u, jnp.where(field == 3, v, x))
    cols_o[...] = jnp.where(even, pltpu.roll(x, 127, 1), pltpu.roll(x, 1, 1))


def final_kernel(
    dims, count, core, projected, part, kry, adj, sten, cw, fwd, back, cols, mine, other,
    out_hbm, comb, low, edges, rim_f, rim_b, out, sem,
):
    vectors, levels, fields, height = dims
    half = vectors // 2
    per = levels * fields
    coupling = [
        jnp.sum(part[k : k + 1], axis=1, keepdims=True) * (1.0 / count) for k in range(vectors)
    ]
    mix = []
    for j in range(vectors):
        m = projected[0, j] * coupling[0]
        for k in range(1, vectors):
            m = m + projected[k, j] * coupling[k]
        mix.append(m)
    is_low = core[0] == 0
    mine_mix = [jnp.where(is_low, mix[k], mix[half + k]) for k in range(half)]
    other_mix = [jnp.where(is_low, mix[half + k], mix[k]) for k in range(half)]

    rim_f[...] = sum(mix[k] * fwd[k * 16 : (k + 1) * 16] for k in range(vectors))
    rim_b[...] = sum(mix[k] * back[k * 16 : (k + 1) * 16] for k in range(vectors))

    step = 64
    chunks = height // step

    def combine(i, carry):
        at = pl.ds(pl.multiple_of(i * step, step), step)
        for c in range(2):
            low[c, at] = sum(
                mine_mix[k] * mine[k, c, at] + other_mix[k] * other[k, c, at] for k in range(half)
            )
        lane = lanes((step, 128)) // (2 * per)
        weight = jnp.zeros((step, 128), F32)
        for k in range(vectors):
            weight = jnp.where(lane == k, mix[k], weight)
        z = cols[at] * weight
        w = z
        for k in range(1, vectors):
            w = w + pltpu.roll(z, 128 - 2 * per * k, 1)
        edges[at] = w
        for l in range(levels):
            for f in range(fields):
                comb[l, f, at] = sum(mix[k] * kry[k, l, f, at].astype(F32) for k in range(vectors))
        return carry

    lax.fori_loop(0, chunks, combine, 0)

    copies = []
    for f in range(fields):

        def stencil(n, carry, f=f):
            l = n // chunks
            i = n % chunks
            at = pl.ds(pl.multiple_of(i * step, step), step)
            before = pl.ds(pl.multiple_of(jnp.maximum(i * step - 16, 0), 16), 16)
            after = pl.ds(pl.multiple_of(jnp.minimum(i * step + step, height - 16), 16), 16)
            q = l * fields + f
            x = comb[l, f, at]
            r = rows((step, 128))
            lane = lanes((step, 128))
            image = sten[0, l, at].astype(F32) * x
            p1 = sten[1, l, at].astype(F32) * x
            head = (sten[1, l, before].astype(F32) * comb[l, f, before])[15:16]
            head = jnp.where(i == 0, rim_f[pl.ds(q, 1)], head)
            image = image + jnp.where(r == 0, head, pltpu.roll(p1, 1, 0))
            p2 = sten[2, l, at].astype(F32) * x
            tail = (sten[2, l, after].astype(F32) * comb[l, f, after])[0:1]
            tail = jnp.where(i == chunks - 1, rim_b[pl.ds(q, 1)], tail)
            image = image + jnp.where(r == step - 1, tail, pltpu.roll(p2, step - 1, 0))
            side = pltpu.roll(edges[at], 127 - 2 * q, 1)
            p3 = sten[3, l, at].astype(F32) * x
            image = image + jnp.where(lane == 0, side, pltpu.roll(p3, 1, 1))
            p4 = sten[4, l, at].astype(F32) * x
            image = image + jnp.where(lane == 127, side, pltpu.roll(p4, 127, 1))
            if f in (1, 4):
                c, source = (0, 0) if f == 1 else (1, 3)
                column = low[c, at]
                for l2 in range(levels):
                    column = column + jnp.where(l2 >= l, comb[l2, source, at], 0.0)
                image = image + cw[c, l, at] * column
            out[l, f, at] = adj[l, f, at] + 0.5 * image
            return carry

        lax.fori_loop(0, levels * chunks, stencil, 0)
        copy = pltpu.make_async_copy(out.at[:, f], out_hbm.at[:, f], sem.at[f])
        copy.start()
        copies.append(copy)
    for copy in copies:
        copy.wait()


def per_device(krylov, adjoint, projected, stencil, column_weight, seam_turns):
    vectors, levels, fields, height, width = krylov.shape
    dims = (vectors, levels, fields, height)
    half = vectors // 2
    tiles, groups = lax.axis_size("tile"), lax.axis_size("lev")
    count = levels * fields * height * width * tiles * groups
    group = lax.axis_index("lev")
    core = (group % 2).astype(jnp.int32).reshape(1)
    params = pltpu.CompilerParams(vmem_limit_bytes=VMEM_LIMIT)
    bf16 = krylov.dtype

    kry, adj, part, mine, theirs = pl.pallas_call(
        functools.partial(dots_kernel, dims),
        out_shape=(
            pltpu.VMEM(krylov.shape, bf16),
            pltpu.VMEM(adjoint.shape, F32),
            pltpu.VMEM((8, 128), F32),
            pltpu.VMEM((half, 2, height, width), F32),
            pltpu.VMEM((half, 2, height, width), F32),
        ),
        in_specs=[IN_SMEM, ANY, ANY],
        out_specs=[IN_VMEM] * 5,
        scratch_shapes=[
            pltpu.VMEM((vectors, 2, height, width), F32),
            pltpu.SemaphoreType.DMA((levels * fields,)),
            pltpu.SemaphoreType.DMA((levels * fields,)),
        ],
        compiler_params=params,
        name="dots",
    )(core, krylov, adjoint)

    first = exchange(theirs, "lev", 1)
    segment = mine + first
    below = jnp.zeros_like(segment)
    for bit in bits("lev")[1:]:
        got = exchange(segment, "lev", bit)
        below = below + jnp.where(group & bit == 0, got, 0.0)
        segment = segment + got
    other = exchange(below + jnp.where(core == 1, mine, 0.0), "lev", 1)
    below = below + jnp.where(core == 0, first, 0.0)

    sten, cw, fwd, back, cols = pl.pallas_call(
        functools.partial(strips_kernel, dims),
        out_shape=(
            pltpu.VMEM(stencil.shape, stencil.dtype),
            pltpu.VMEM(column_weight.shape, F32),
            pltpu.VMEM((vectors * 16, width), F32),
            pltpu.VMEM((vectors * 16, width), F32),
            pltpu.VMEM((height, width), F32),
        ),
        in_specs=[IN_VMEM, ANY, ANY],
        out_specs=[IN_VMEM] * 5,
        scratch_shapes=[pltpu.SemaphoreType.DMA((2,))],
        compiler_params=params,
        name="strips",
    )(pinned(kry), stencil, column_weight)

    for bit in bits("lev")[1:]:
        part = part + exchange(part, "lev", bit)
    part = part + exchange(part, "lev", 1)
    for bit in bits("tile"):
        part = part + exchange(part, "tile", bit)

    up = shifted(cols, "tile", STRIDE)
    down = up if (2 * STRIDE) % tiles == 0 else shifted(cols, "tile", -STRIDE)
    fwd = shifted(fwd, "tile", 1)
    back = shifted(back, "tile", -1)
    fwd, back, cols = pl.pallas_call(
        functools.partial(turn_kernel, dims),
        out_shape=(
            pltpu.VMEM(fwd.shape, F32),
            pltpu.VMEM(back.shape, F32),
            pltpu.VMEM(cols.shape, F32),
        ),
        in_specs=[IN_SMEM] + [IN_VMEM] * 4,
        out_specs=[IN_VMEM] * 3,
        compiler_params=params,
        name="turn",
    )(seam_turns, pinned(fwd), pinned(back), pinned(up), pinned(down))

    return pl.pallas_call(
        functools.partial(final_kernel, dims, count),
        out_shape=jax.ShapeDtypeStruct(adjoint.shape, F32),
        in_specs=[IN_SMEM, IN_SMEM] + [IN_VMEM] * 10,
        out_specs=ANY,
        scratch_shapes=[
            pltpu.VMEM((levels, fields, height, width), F32),
            pltpu.VMEM((2, height, width), F32),
            pltpu.VMEM((height, width), F32),
            pltpu.VMEM((16, width), F32),
            pltpu.VMEM((16, width), F32),
            pltpu.VMEM((levels, fields, height, width), F32),
            pltpu.SemaphoreType.DMA((fields,)),
        ],
        compiler_params=params,
        name="final",
    )(
        core, projected, pinned(part), pinned(kry), pinned(adj), pinned(sten), pinned(cw),
        pinned(fwd), pinned(back), pinned(cols), pinned(below), pinned(other),
    )


def solution(mesh):
    placed = (
        P(None, "lev", None, "tile", None),
        P("lev", None, "tile", None),
        P(),
        P(None, "lev", "tile", None),
        P(None, "lev", "tile", None),
        P("tile", None),
    )
    return jax.shard_map(
        per_device,
        mesh=mesh,
        in_specs=placed,
        out_specs=P("lev", None, "tile", None),
        check_vma=False,
    )
```

time: 158 us -> 61.4 us (0.39)
  blocking collectives: 40.3 us -> 0 us
  other arithmetic: 38.6 us -> 2.29 us
  local copies, waits for them, and re-layouts: 38 us -> 4.97 us
  between operations: 31.4 us -> 0.11 us
  waiting for transfers between devices: 0.03 us -> 29.2 us
  Pallas kernels: 0 us -> 12.3 us
  starting transfers between devices: 8.9 us -> 12.4 us
    psum x1 -> x0, blocking collectives: 40.3 us -> none  [per_device(): coupling = lax.psum(partial_value, ('tile', 'lev')) / count]
    ppermute x4 -> x11, waiting for transfers between devices: 0.01 us -> 29.2 us  [the longest x8 29.2 us: exchange(): return lax.ppermute(x, axis, [(i, i ^ bit) for i in range(size)])]
    slice x12 -> x0, local copies, waits for them, and re-layouts: 24.7 us -> none  [the longest x2 9.72 us: apply_operator(): up_strip = shifted(plus_cols[..., -1], 'tile', STRIDE)]
    reduce_sum x4 -> x0, other arithmetic: 24.5 us -> none  [the longest x1 11.2 us: per_device(): partial_value = jnp.sum(vectors * adjoint[None], axis=(1, 2, 3, 4))]
    pallas_call x0 -> x4, Pallas kernels: none -> 12.3 us  [the longest x1 6.26 us: per_device(): pl.pallas_call(functools.partial(final_kernel, dims, count), out_shape=ja...]
    select_n x8 -> x0, other arithmetic: 6.42 us -> none  [the longest x4 6.34 us: step(): return jnp.where(reached, new, before)]
    broadcast_in_dim x4 -> x0, local copies, waits for them, and re-layouts: 6.3 us -> none  [the longest x1 3.19 us: apply_operator(): down_strip[..., None]]
    ppermute x4 -> x11, starting transfers between devices: 8.89 us -> 12.4 us  [the longest x3 7.6 us: shifted(): return lax.ppermute(x, axis, [(i, (i + steps) % size) for i in range(size)])]
  transfers between devices with their start and end apart: 5 -> 11, of which waited for: 0 -> 7; matrix products, arithmetic and copies ran while one was open for 32% -> 0% of each run, Pallas kernels for 0% -> 5%
where the time goes in v1:
time: 61.4 us; the launch traced here: 61.2 us
  waiting for transfers between devices  29.2 us (48%)
  starting transfers between devices  12.4 us (20%)
  Pallas kernels  12.3 us (20%)
  local copies, waits for them, and re-layouts  4.97 us (8%)
  other arithmetic  2.29 us (4%)
    ppermute x8, waiting for transfers between devices, exchange(): return lax.ppermute(x, axis, [(i, i ^ bit) for i in range(size)])  29.2 us
    ppermute x3, starting transfers between devices, shifted(): return lax.ppermute(x, axis, [(i, (i + steps) % size) for i in range(size)])  7.6 us
    pallas_call x1, Pallas kernels, per_device(): pl.pallas_call(functools.partial(final_kernel, dims, count), out_shape=ja...  6.26 us
    unnamed x18, local copies, waits for them, and re-layouts  4.97 us
    ppermute x8, starting transfers between devices, exchange(): return lax.ppermute(x, axis, [(i, i ^ bit) for i in range(size)])  4.78 us
    pallas_call x1, Pallas kernels, per_device(): pl.pallas_call(functools.partial(dots_kernel, dims), out_shape=(pltpu.VME...  3.22 us
    pallas_call x1, Pallas kernels, per_device(): pl.pallas_call(functools.partial(strips_kernel, dims), out_shape=(pltpu.V...  1.63 us
    add x1, other arithmetic, per_device(): other = exchange(below + jnp.where(core == 1, mine, 0.0), 'lev', 1)  1.42 us
  transfers between devices with their start and end apart: 11, of which 7 were waited for; matrix products, arithmetic and copies ran while one was open for 0% of the time, Pallas kernels for 5%

profile of v1, /device:TPU:0, one launch (start us, length us, event | category | flops | bytes accessed | tf_op | source)
XLA Modules:
  0.0 61.2 jit_solution(5774001611834421748)
XLA Ops:
  0.0 0.0 copy-start
  0.0 1.7 %copy-done = bf16[4,2,5,256,128]{4,3,2,1,0:T(8,128)(2,1)S(1)} copy-done((bf16[4,2,5,256,128]{4,3,2,1,0:T(8,128)(2,1)S(1)}, bf16[4,2,5,256,128]{4,3,2,1,0:T(8,128)(2,1)}, u32[]{:S(2)}) %copy-start) | copy-done | bytes 2621464
  1.7 0.0 copy-start.1
  1.7 1.3 %copy-done.1 = f32[2,5,256,128]{3,2,1,0:T(8,128)S(1)} copy-done((f32[2,5,256,128]{3,2,1,0:T(8,128)S(1)}, f32[2,5,256,128]{3,2,1,0:T(8,128)}, u32[]{:S(2)}) %copy-start.1) | copy-done | bytes 1310744
  3.1 3.2 %dots.1 = (bf16[4,2,5,256,128]{4,3,2,1,0:T(8,128)(2,1)S(1)}, f32[2,5,256,128]{3,2,1,0:T(8,128)S(1)}, f32[8,128]{1,0:T(8,128)S(1)}, f32[2,2,256,128]{3,2,1,0:T(8,128)S(1)}, f32[2,2,256,128]{3,2,1,0:T(8,128)S(1)}) custom-call(s32[1]{0:T(128)} %bitcast.core, bf16[4,2,5,256,128]{4,3,2,1,0:T(8,128)(2,1)S(1)} %copy-done, f32[2,5,256,128]{3,2,1,0:T(8,128)S(1)} %copy-done.1), custom_call_target="tpu_custom_call" | custom-call | tf_op jit(solution)/shard_map/dots/pallas_call | solution.py:299
  6.3 0.0 copy-start.2
  6.3 1.0 %copy-done.2 = f32[2,5,256,128]{3,2,1,0:T(8,128)} copy-done((f32[2,5,256,128]{3,2,1,0:T(8,128)}, f32[2,5,256,128]{3,2,1,0:T(8,128)S(1)}, u32[]{:S(2)}) %copy-start.2) | copy-done | bytes 1310744
  7.3 0.5 collective-permute-start.8
  7.8 1.5 %collective-permute-done.8 = f32[2,2,256,128]{3,2,1,0:T(8,128)S(1)} collective-permute-done((f32[2,2,256,128]{3,2,1,0:T(8,128)S(1)}, f32[2,2,256,128]{3,2,1,0:T(8,128)S(1)}, u32[]{:S(2)}, u32[]{:S(2)}) %collective-permute-start.8) | collective-permute-done | bytes 524320 | tf_op jit(solution)/shard_map/ppermute | solution.py:25
  9.3 0.0 copy-start.8
  9.3 0.8 %copy-done.8 = f32[2,2,256,128]{3,2,1,0:T(8,128)} copy-done((f32[2,2,256,128]{3,2,1,0:T(8,128)}, f32[2,2,256,128]{3,2,1,0:T(8,128)S(1)}, u32[]{:S(2)}) %copy-start.8) | copy-done | bytes 524312
  10.1 0.9 %add.34 = f32[2,2,256,128]{3,2,1,0:T(8,128)} add(f32[2,2,256,128]{3,2,1,0:T(8,128)S(1)} %get-tuple-element.29, f32[2,2,256,128]{3,2,1,0:T(8,128)S(1)} %collective-permute-done.8) | non-fusion elementwise | flops 131072 | bytes 1572864 | tf_op jit(solution)/shard_map/add | solution.py:320
  11.0 2.9 %collective-permute-start.9 = (f32[2,2,256,128]{3,2,1,0:T(8,128)}, f32[2,2,256,128]{3,2,1,0:T(8,128)}, u32[]{:S(2)}, u32[]{:S(2)}) collective-permute-start(f32[2,2,256,128]{3,2,1,0:T(8,128)} %add.34), channel_id=1, source_target_pairs={{0,2},{1,3},{2,0},{3,1},{4,6},{5,7},{6,4},{7,5},{8,10},{9,11},{10,... | collective-permute-start | bytes 1572872 | tf_op jit(solution)/shard_map/ppermute | solution.py:25
  13.9 12.5 %collective-permute-done.9 = f32[2,2,256,128]{3,2,1,0:T(8,128)} collective-permute-done((f32[2,2,256,128]{3,2,1,0:T(8,128)}, f32[2,2,256,128]{3,2,1,0:T(8,128)}, u32[]{:S(2)}, u32[]{:S(2)}) %collective-permute-start.9) | collective-permute-done | bytes 524320 | tf_op jit(solution)/shard_map/ppermute | solution.py:25
  26.4 0.0 copy-start.4
  26.4 0.0 copy-start.5
  26.4 1.4 %select_add_fusion = (f32[2,2,256,128]{3,2,1,0:T(8,128)S(1)}, f32[2,2,256,128]{3,2,1,0:T(8,128)S(1)}) fusion(f32[2,2,256,128]{3,2,1,0:T(8,128)S(1)} %get-tuple-element.29, f32[2,2,256,128]{3,2,1,0:T(8,128)} %collective-permute-done.9, pred[]{:T(512)} %bitcast.2, pred[]{:T(512)S(6)} %eq.15, f32[2,2,256,128]{3,2,1,0:T(8,128)} %copy-done.8, pred[]{:T(512)} %bitcast.1), kind=kLoop, calls=%fused_computation | loop fusion | flops 655360 | bytes 2621443 | tf_op jit(solution)/shard_map/add | solution.py:326
  27.8 0.1 collective-permute-start.10
  27.9 0.0 copy-done.4
  27.9 0.0 copy-done.5
  28.0 0.0 copy-start.7
  28.0 0.0 copy-start.3
  28.0 0.0 copy-start.6
  28.0 1.6 %strips.1 = (bf16[5,2,256,128]{3,2,1,0:T(8,128)(2,1)S(1)}, f32[2,2,256,128]{3,2,1,0:T(8,128)S(1)}, f32[64,128]{1,0:T(8,128)S(1)}, f32[64,128]{1,0:T(8,128)S(1)}, f32[256,128]{1,0:T(8,128)S(1)}) custom-call(bf16[4,2,5,256,128]{4,3,2,1,0:T(8,128)(2,1)S(1)} %get-tuple-element.19.kry_v.kry, bf16[5,2,256,128]{3,2,1,0:T(8,128)(2,1)S(1)} %copy-done.4, ...), custom_call_target="tpu_custom_call" | custom-call | tf_op jit(solution)/shard_map/strips/pallas_call | solution.py:329
  29.6 2.9 %collective-permute-start.7 = (f32[256,128]{1,0:T(8,128)S(1)}, f32[256,128]{1,0:T(8,128)S(1)}, u32[]{:S(2)}, u32[]{:S(2)}) collective-permute-start(f32[256,128]{1,0:T(8,128)S(1)} %get-tuple-element.25), channel_id=1, source_target_pairs={{0,16},{4,20},{8,24},{12,28},{16,0},{20,4},{24,8},{28,12},{1,17},{... | collective-permute-start | bytes 393224 | tf_op jit(solution)/shard_map/ppermute | solution.py:30
  32.5 1.5 %collective-permute-start.5 = (f32[64,128]{1,0:T(8,128)S(1)}, f32[64,128]{1,0:T(8,128)S(1)}, u32[]{:S(2)}, u32[]{:S(2)}) collective-permute-start(f32[64,128]{1,0:T(8,128)S(1)} %get-tuple-element.23), channel_id=1, source_target_pairs={{0,4},{4,8},{8,12},{12,16},{16,20},{20,24},{24,28},{28,0},{1,5},{5... | collective-permute-start | bytes 98312 | tf_op jit(solution)/shard_map/ppermute | solution.py:30
  34.0 3.2 %collective-permute-start.6 = (f32[64,128]{1,0:T(8,128)S(1)}, f32[64,128]{1,0:T(8,128)S(1)}, u32[]{:S(2)}, u32[]{:S(2)}) collective-permute-start(f32[64,128]{1,0:T(8,128)S(1)} %get-tuple-element.24), channel_id=1, source_target_pairs={{0,28},{4,0},{8,4},{12,8},{16,12},{20,16},{24,20},{28,24},{1,29},{... | collective-permute-start | bytes 98312 | tf_op jit(solution)/shard_map/ppermute | solution.py:30
  37.2 1.4 %collective-permute-start = (f32[8,128]{1,0:T(8,128)S(1)}, f32[8,128]{1,0:T(8,128)S(1)}, u32[]{:S(2)}, u32[]{:S(2)}) collective-permute-start(f32[8,128]{1,0:T(8,128)S(1)} %get-tuple-element.18), channel_id=1, source_target_pairs={{0,2},{1,3},{2,0},{3,1},{4,6},{5,7},{6,4},{7,5},{8,10},{9,11},{10,... | collective-permute-start | bytes 12296 | tf_op jit(solution)/shard_map/ppermute | solution.py:25
  38.6 2.2 %collective-permute-done = f32[8,128]{1,0:T(8,128)S(1)} collective-permute-done((f32[8,128]{1,0:T(8,128)S(1)}, f32[8,128]{1,0:T(8,128)S(1)}, u32[]{:S(2)}, u32[]{:S(2)}) %collective-permute-start) | collective-permute-done | bytes 4128 | tf_op jit(solution)/shard_map/ppermute | solution.py:25
  40.8 0.0 collective-permute-start.1
  40.8 1.2 %collective-permute-done.1 = f32[8,128]{1,0:T(8,128)S(1)} collective-permute-done((f32[8,128]{1,0:T(8,128)S(1)}, f32[8,128]{1,0:T(8,128)S(1)}, u32[]{:S(2)}, u32[]{:S(2)}) %collective-permute-start.1) | collective-permute-done | bytes 4128 | tf_op jit(solution)/shard_map/ppermute | solution.py:25
  42.0 0.0 collective-permute-start.2
  42.0 3.6 %collective-permute-done.2 = f32[8,128]{1,0:T(8,128)S(1)} collective-permute-done((f32[8,128]{1,0:T(8,128)S(1)}, f32[8,128]{1,0:T(8,128)S(1)}, u32[]{:S(2)}, u32[]{:S(2)}) %collective-permute-start.2) | collective-permute-done | bytes 4128 | tf_op jit(solution)/shard_map/ppermute | solution.py:25
  45.6 0.0 collective-permute-start.3
  45.6 3.6 %collective-permute-done.3 = f32[8,128]{1,0:T(8,128)S(1)} collective-permute-done((f32[8,128]{1,0:T(8,128)S(1)}, f32[8,128]{1,0:T(8,128)S(1)}, u32[]{:S(2)}, u32[]{:S(2)}) %collective-permute-start.3) | collective-permute-done | bytes 4128 | tf_op jit(solution)/shard_map/ppermute | solution.py:25
  49.2 0.0 collective-permute-start.4
  49.2 4.5 %collective-permute-done.4 = f32[8,128]{1,0:T(8,128)S(1)} collective-permute-done((f32[8,128]{1,0:T(8,128)S(1)}, f32[8,128]{1,0:T(8,128)S(1)}, u32[]{:S(2)}, u32[]{:S(2)}) %collective-permute-start.4) | collective-permute-done | bytes 4128 | tf_op jit(solution)/shard_map/ppermute | solution.py:25
  53.7 0.0 collective-permute-done.5.fwd
  53.7 0.0 collective-permute-done.6.back
  53.7 0.0 collective-permute-done.7.up.down
  53.7 0.0 copy-done.7
  53.8 1.2 %turn.1 = (f32[64,128]{1,0:T(8,128)S(1)}, f32[64,128]{1,0:T(8,128)S(1)}, f32[256,128]{1,0:T(8,128)S(1)}) custom-call(s32[1,4]{1,0:T(1,128)S(1)} %copy-done.7, f32[64,128]{1,0:T(8,128)S(1)} %collective-permute-done.5.fwd, f32[64,128]{1,0:T(8,128)S(1)} %collective-permute-done.6.back, f32[256,128]{1,0:T(8,128)S(1)} %collective-permute-done.7.up.down, ...), custom_call_target="tpu_custom_call" | custom-call | tf_op jit(solution)/shard_map/turn/pallas_call | solution.py:355
  54.9 0.0 collective-permute-done.10.other
  54.9 0.0 copy-done.3
  55.0 0.0 copy-done.6
  55.0 6.3 %final.1 = f32[2,5,256,128]{3,2,1,0:T(8,128)} custom-call(s32[1]{0:T(128)} %bitcast.core, f32[4,4]{1,0:T(4,128)S(1)} %copy-done.6, f32[8,128]{1,0:T(8,128)S(1)} %add.33.part, bf16[4,2,5,256,128]{4,3,2,1,0:T(8,128)(2,1)S(1)} %get-tuple-element.19.kry_v.kry, f32[2,5,256,128]{3,2,1,0:T(8,128)S(1)} %copy-done.3, ...), custom_call_target="tpu_custom_call" | custom-call | tf_op jit(solution)/shard_map/final/pallas_call | solution.py:368
  (5 shorter events, 0.0 us)
Async XLA Ops:
  0.0 1.7 %copy-start = (bf16[4,2,5,256,128]{4,3,2,1,0:T(8,128)(2,1)S(1)}, bf16[4,2,5,256,128]{4,3,2,1,0:T(8,128)(2,1)}, u32[]{:S(2)}) copy-start(bf16[4,2,5,256,128]{4,3,2,1,0:T(8,128)(2,1)} %kry.1) | copy-start | bytes 7864324
  1.7 1.3 %copy-start.1 = (f32[2,5,256,128]{3,2,1,0:T(8,128)S(1)}, f32[2,5,256,128]{3,2,1,0:T(8,128)}, u32[]{:S(2)}) copy-start(f32[2,5,256,128]{3,2,1,0:T(8,128)} %adj.1) | copy-start | bytes 3932164
  6.3 1.1 %copy-start.2 = (f32[2,5,256,128]{3,2,1,0:T(8,128)}, f32[2,5,256,128]{3,2,1,0:T(8,128)S(1)}, u32[]{:S(2)}) copy-start(f32[2,5,256,128]{3,2,1,0:T(8,128)S(1)} %get-tuple-element.20.adj) | copy-start | bytes 3932164
  7.3 2.0 %collective-permute-start.8 = (f32[2,2,256,128]{3,2,1,0:T(8,128)S(1)}, f32[2,2,256,128]{3,2,1,0:T(8,128)S(1)}, u32[]{:S(2)}, u32[]{:S(2)}) collective-permute-start(f32[2,2,256,128]{3,2,1,0:T(8,128)S(1)} %get-tuple-element.30), channel_id=1, source_target_pairs={{0,1},{1,0},{2,3},{3,2},{4,5},{5,4},{6,7},{7,6},{8,9},{9,8},{10,11... | collective-permute-start | bytes 1572872 | tf_op jit(solution)/shard_map/ppermute | solution.py:25
  9.3 0.8 %copy-start.8 = (f32[2,2,256,128]{3,2,1,0:T(8,128)}, f32[2,2,256,128]{3,2,1,0:T(8,128)S(1)}, u32[]{:S(2)}) copy-start(f32[2,2,256,128]{3,2,1,0:T(8,128)S(1)} %collective-permute-done.8) | copy-start | bytes 1572868
  11.0 15.4 %collective-permute-start.9 = (f32[2,2,256,128]{3,2,1,0:T(8,128)}, f32[2,2,256,128]{3,2,1,0:T(8,128)}, u32[]{:S(2)}, u32[]{:S(2)}) collective-permute-start(f32[2,2,256,128]{3,2,1,0:T(8,128)} %add.34), channel_id=1, source_target_pairs={{0,2},{1,3},{2,0},{3,1},{4,6},{5,7},{6,4},{7,5},{8,10},{9,11},{10,... | collective-permute-start | bytes 1572872 | tf_op jit(solution)/shard_map/ppermute | solution.py:25
  26.4 1.5 %copy-start.4 = (bf16[5,2,256,128]{3,2,1,0:T(8,128)(2,1)S(1)}, bf16[5,2,256,128]{3,2,1,0:T(8,128)(2,1)}, u32[]{:S(2)}) copy-start(bf16[5,2,256,128]{3,2,1,0:T(8,128)(2,1)} %sten.1) | copy-start | bytes 1966084
  26.4 1.6 %copy-start.5 = (f32[2,2,256,128]{3,2,1,0:T(8,128)S(1)}, f32[2,2,256,128]{3,2,1,0:T(8,128)}, u32[]{:S(2)}) copy-start(f32[2,2,256,128]{3,2,1,0:T(8,128)} %cw.1) | copy-start | bytes 1572868
  27.8 27.1 %collective-permute-start.10 = (f32[2,2,256,128]{3,2,1,0:T(8,128)S(1)}, f32[2,2,256,128]{3,2,1,0:T(8,128)S(1)}, u32[]{:S(2)}, u32[]{:S(2)}) collective-permute-start(f32[2,2,256,128]{3,2,1,0:T(8,128)S(1)} %get-tuple-element.31), channel_id=1, source_target_pairs={{0,1},{1,0},{2,3},{3,2},{4,5},{5,4},{6,7},{7,6},{8,9},{9,8},{10,11... | collective-permute-start | bytes 1572872 | tf_op jit(solution)/shard_map/ppermute | solution.py:25
  28.0 25.8 %copy-start.7 = (s32[1,4]{1,0:T(1,128)S(1)}, s32[1,4]{1,0:T(1,128)}, u32[]{:S(2)}) copy-start(s32[1,4]{1,0:T(1,128)} %turns.1) | copy-start | bytes 52
  28.0 27.0 %copy-start.3 = (f32[2,5,256,128]{3,2,1,0:T(8,128)S(1)}, f32[2,5,256,128]{3,2,1,0:T(8,128)}, u32[]{:S(2)}) copy-start(f32[2,5,256,128]{3,2,1,0:T(8,128)} %copy-done.2) | copy-start | bytes 3932164
  28.0 27.0 %copy-start.6 = (f32[4,4]{1,0:T(4,128)S(1)}, f32[4,4]{1,0:T(4,128)}, u32[]{:S(2)}) copy-start(f32[4,4]{1,0:T(4,128)} %projected.1) | copy-start | bytes 196
  29.6 24.1 %collective-permute-start.7 = (f32[256,128]{1,0:T(8,128)S(1)}, f32[256,128]{1,0:T(8,128)S(1)}, u32[]{:S(2)}, u32[]{:S(2)}) collective-permute-start(f32[256,128]{1,0:T(8,128)S(1)} %get-tuple-element.25), channel_id=1, source_target_pairs={{0,16},{4,20},{8,24},{12,28},{16,0},{20,4},{24,8},{28,12},{1,17},{... | collective-permute-start | bytes 393224 | tf_op jit(solution)/shard_map/ppermute | solution.py:30
  32.5 21.2 %collective-permute-start.5 = (f32[64,128]{1,0:T(8,128)S(1)}, f32[64,128]{1,0:T(8,128)S(1)}, u32[]{:S(2)}, u32[]{:S(2)}) collective-permute-start(f32[64,128]{1,0:T(8,128)S(1)} %get-tuple-element.23), channel_id=1, source_target_pairs={{0,4},{4,8},{8,12},{12,16},{16,20},{20,24},{24,28},{28,0},{1,5},{5... | collective-permute-start | bytes 98312 | tf_op jit(solution)/shard_map/ppermute | solution.py:30
  34.0 19.8 %collective-permute-start.6 = (f32[64,128]{1,0:T(8,128)S(1)}, f32[64,128]{1,0:T(8,128)S(1)}, u32[]{:S(2)}, u32[]{:S(2)}) collective-permute-start(f32[64,128]{1,0:T(8,128)S(1)} %get-tuple-element.24), channel_id=1, source_target_pairs={{0,28},{4,0},{8,4},{12,8},{16,12},{20,16},{24,20},{28,24},{1,29},{... | collective-permute-start | bytes 98312 | tf_op jit(solution)/shard_map/ppermute | solution.py:30
  37.2 3.6 %collective-permute-start = (f32[8,128]{1,0:T(8,128)S(1)}, f32[8,128]{1,0:T(8,128)S(1)}, u32[]{:S(2)}, u32[]{:S(2)}) collective-permute-start(f32[8,128]{1,0:T(8,128)S(1)} %get-tuple-element.18), channel_id=1, source_target_pairs={{0,2},{1,3},{2,0},{3,1},{4,6},{5,7},{6,4},{7,5},{8,10},{9,11},{10,... | collective-permute-start | bytes 12296 | tf_op jit(solution)/shard_map/ppermute | solution.py:25
  40.8 1.2 %collective-permute-start.1 = (f32[8,128]{1,0:T(8,128)S(1)}, f32[8,128]{1,0:T(8,128)S(1)}, u32[]{:S(2)}, u32[]{:S(2)}) collective-permute-start(f32[8,128]{1,0:T(8,128)S(1)} %add.29), channel_id=1, source_target_pairs={{0,1},{1,0},{2,3},{3,2},{4,5},{5,4},{6,7},{7,6},{8,9},{9,8},{10,11... | collective-permute-start | bytes 12296 | tf_op jit(solution)/shard_map/ppermute | solution.py:25
  42.0 3.6 %collective-permute-start.2 = (f32[8,128]{1,0:T(8,128)S(1)}, f32[8,128]{1,0:T(8,128)S(1)}, u32[]{:S(2)}, u32[]{:S(2)}) collective-permute-start(f32[8,128]{1,0:T(8,128)S(1)} %add.30), channel_id=1, source_target_pairs={{0,4},{4,0},{8,12},{12,8},{16,20},{20,16},{24,28},{28,24},{1,5},{5... | collective-permute-start | bytes 12296 | tf_op jit(solution)/shard_map/ppermute | solution.py:25
  45.6 3.6 %collective-permute-start.3 = (f32[8,128]{1,0:T(8,128)S(1)}, f32[8,128]{1,0:T(8,128)S(1)}, u32[]{:S(2)}, u32[]{:S(2)}) collective-permute-start(f32[8,128]{1,0:T(8,128)S(1)} %add.31), channel_id=1, source_target_pairs={{0,8},{4,12},{8,0},{12,4},{16,24},{20,28},{24,16},{28,20},{1,9},{5... | collective-permute-start | bytes 12296 | tf_op jit(solution)/shard_map/ppermute | solution.py:25
  49.2 4.5 %collective-permute-start.4 = (f32[8,128]{1,0:T(8,128)S(1)}, f32[8,128]{1,0:T(8,128)S(1)}, u32[]{:S(2)}, u32[]{:S(2)}) collective-permute-start(f32[8,128]{1,0:T(8,128)S(1)} %add.32), channel_id=1, source_target_pairs={{0,16},{4,20},{8,24},{12,28},{16,0},{20,4},{24,8},{28,12},{1,17},{... | collective-permute-start | bytes 12296 | tf_op jit(solution)/shard_map/ppermute | solution.py:25

commit v2 on v0

v2 whole, which is shorter than its diff:
```python
import functools

import jax
import jax.numpy as jnp
from jax import lax
from jax.experimental import pallas as pl
from jax.experimental.pallas import tpu as pltpu
from jax.sharding import PartitionSpec as P

STRIDE = 4
F32 = jnp.float32
SMALL = 4 * 1024 * 1024
LARGE = 8 * 1024 * 1024

IN_HBM = pl.BlockSpec(memory_space=pltpu.HBM)
IN_VMEM = pl.BlockSpec(memory_space=pltpu.VMEM)


def pinned(x):
    return pltpu.with_memory_space_constraint(x, pltpu.VMEM)


def in_hbm(x):
    return pltpu.with_memory_space_constraint(x, pltpu.HBM)


def exchange(x, axis, bit):
    size = lax.axis_size(axis)
    return lax.ppermute(x, axis, [(i, i ^ bit) for i in range(size)])


def shifted(x, axis, steps):
    size = lax.axis_size(axis)
    return lax.ppermute(x, axis, [(i, (i + steps) % size) for i in range(size)])


def bits(axis):
    size = lax.axis_size(axis)
    return [1 << b for b in range(size.bit_length() - 1)]


def lanes(shape):
    return lax.broadcasted_iota(jnp.int32, shape, len(shape) - 1)


def rows(shape):
    return lax.broadcasted_iota(jnp.int32, shape, len(shape) - 2)


def bf16(x):
    return x.astype(jnp.bfloat16)


def ends_to(last, first):
    row, lane = rows((16, 128)), lanes((16, 128))
    top = bf16(jnp.where((row == 0) & first(lane), 1.0, 0.0))
    bottom = bf16(jnp.where((row == 15) & last(lane), 1.0, 0.0))
    return jnp.concatenate([top, jnp.zeros((96, 128), jnp.bfloat16), bottom], axis=0)


def dots_kernel(
    dims, count, projected, kry, adj, kry_v, pack, mine, adj_v, proj_v, mixer, sem_k, sem_a, sem_p
):
    vectors, levels, fields, height = dims
    half = vectors // 2
    upper = lax.axis_index("lev") & 1 == 1
    order = [0, 3] + [f for f in range(fields) if f not in (0, 3)]
    copy_p = pltpu.make_async_copy(projected, proj_v, sem_p)
    copy_p.start()
    copies = {}
    for f in order:
        copies[f] = (
            pltpu.make_async_copy(kry.at[:, :, f], kry_v.at[:, :, f], sem_k.at[f]),
            pltpu.make_async_copy(adj.at[:, f], adj_v.at[:, f], sem_a.at[f]),
        )
        for copy in copies[f]:
            copy.start()
    copy_p.wait()
    r = rows((8, 128))
    for k in range(vectors):
        m = jnp.zeros((8, 128), F32)
        for j in range(vectors):
            m = jnp.where(r == j, proj_v[k : k + 1, j : j + 1] * (0.5 / count), m)
        mixer[k] = m
    step = 128
    accs = [jnp.zeros((8, 128), F32) for _ in range(vectors)]
    for f in order:
        for copy in copies[f]:
            copy.wait()
        for l in range(levels):

            def body(i, accs, f=f, l=l):
                start = pl.multiple_of(i * step, step)
                at = pl.ds(start, step)
                y = adj_v[l, f, at]
                out = []
                for k in range(vectors):
                    x = kry_v[k, l, f, at].astype(F32)
                    if f in (0, 3):
                        c = 0 if f == 0 else 1
                        to = pl.ds(start + ((k % half) * 2 + c) * height, step)

                        def put(ref, x=x, to=to):
                            if l == 0:
                                ref[to] = x
                            else:
                                ref[to] = ref[to] + x

                        first, second = (mine, pack) if k < half else (pack, mine)
                        pl.when(jnp.logical_not(upper))(functools.partial(put, first))
                        pl.when(upper)(functools.partial(put, second))
                    p = x * y
                    out.append(accs[k] + jnp.sum(p.reshape(step // 8, 8, 128), axis=0))
                return out

            accs = lax.fori_loop(0, height // step, body, accs)
    total = jnp.zeros((8, 128), F32)
    for k in range(vectors):
        total = total + mixer[k] * jnp.sum(accs[k], axis=0, keepdims=True)
    pack[vectors * height : vectors * height + 8] = total


def strips_kernel(dims, kry_v, sten, sten_v, near, far, cols, sem):
    vectors, levels, fields, height = dims
    per = levels * fields
    even_tile = lax.axis_index("tile") & 1 == 0
    copy = pltpu.make_async_copy(sten, sten_v, sem)
    copy.start()
    near[...] = jnp.zeros_like(near)
    far[...] = jnp.zeros_like(far)
    planes = [(k, l, f) for k in range(vectors) for l in range(levels) for f in range(fields)]
    cols[...] = jnp.dot(
        jnp.concatenate([kry_v[p] for p in planes], axis=1),
        jnp.concatenate(
            [
                ends_to(lambda lane, s=2 * s: lane == s, lambda lane, s=2 * s: lane == s + 1)
                for s in range(len(planes))
            ],
            axis=0,
        ),
        preferred_element_type=F32,
    )
    copy.wait()
    tail = height - 16
    for l in range(levels):
        last = sten_v[1, l, tail:height].astype(F32)
        first = sten_v[2, l, 0:16].astype(F32)
        for k in range(vectors):
            for f in range(fields):
                s = k * 16 + l * fields + f
                fwd = (kry_v[k, l, f, tail:height].astype(F32) * last)[15:16]
                back = (kry_v[k, l, f, 0:16].astype(F32) * first)[0:1]
                near[8 + s : 9 + s] = jnp.where(even_tile, fwd, back)
                far[s : s + 1] = jnp.where(even_tile, back, fwd)
    none = lambda lane: lane < 0
    weights = []
    for l in range(levels):
        here = lambda lane, l=l: lane % (2 * per) // (2 * fields) == l
        weights.append(ends_to(lambda lane, here=here: here(lane) & (lane % 2 == 0), none))
        weights.append(ends_to(none, lambda lane, here=here: here(lane) & (lane % 2 == 1)))
    coeff = jnp.dot(
        jnp.concatenate([sten_v[d, l] for l in range(levels) for d in (3, 4)], axis=1),
        jnp.concatenate(weights, axis=0),
        preferred_element_type=F32,
    )
    cols[...] = cols[...] * coeff


def turn_of(r):
    cosine = jnp.where(r == 0, 1.0, jnp.where(r == 2, -1.0, 0.0)).astype(F32)
    sine = jnp.where(r == 1, 1.0, jnp.where(r == 3, -1.0, 0.0)).astype(F32)
    return cosine, sine


def turn_kernel(dims, turns, near, far, up, down, fwd_o, back_o, cols_o):
    vectors, levels, fields, height = dims
    per = levels * fields
    n = vectors * 16
    flip = (lanes((128, 128)) + rows((128, 128)) == 127).astype(F32)
    r = rows((n, 128)) % 16
    field = r % fields
    real = r < per
    even_tile = lax.axis_index("tile") & 1 == 0
    for side, out in ((0, fwd_o), (1, back_o)):
        turning = jnp.broadcast_to(turns[0:1, side : side + 1], (n, 128))
        first, second = (far[...], near[8:]) if side == 0 else (near[8:], far[...])
        x = jnp.where(even_tile, first, second)
        x = jnp.where(
            turning % 2 == 1,
            jnp.dot(x, flip, precision=lax.Precision.HIGHEST, preferred_element_type=F32),
            x,
        )
        cosine, sine = turn_of(turning)
        u = cosine * x - sine * pltpu.roll(x, n - 1, 0)
        v = sine * pltpu.roll(x, 1, 0) + cosine * x
        out[...] = jnp.where(real & (field == 2), u, jnp.where(real & (field == 3), v, x))
    lane = lanes((height, 128))
    even = lane % 2 == 0
    x = jnp.where(even, up[...], down[...])
    mirror = (lanes((height, height)) + rows((height, height)) == height - 1).astype(F32)
    mirrored = jnp.dot(mirror, x, precision=lax.Precision.HIGHEST, preferred_element_type=F32)
    turning = jnp.where(lanes((1, 128)) % 2 == 0, turns[0:1, 2:3], turns[0:1, 3:4])
    x = jnp.where(turning % 2 == 1, mirrored, x)
    cosine, sine = turn_of(turning)
    field = lane % (2 * fields) // 2
    u = cosine * x - sine * pltpu.roll(x, 126, 1)
    v = sine * pltpu.roll(x, 2, 1) + cosine * x
    cols_o[...] = jnp.where(field == 2, u, jnp.where(field == 3, v, x))


def tables_kernel(dims, sten, cw, token, coefs, shift, spots, cw_v, sem):
    del token
    vectors, levels, fields, height = dims
    per = levels * fields
    copy = pltpu.make_async_copy(cw, cw_v, sem)
    copy.start()
    row, lane = rows((128, 256)), lanes((128, 256))
    move = bf16(jnp.where((lane == row + 1) & (row < 127) | (lane == row + 127) & (row > 0), 1.0, 0.0))
    shift[0:128] = move
    shift[128:256] = move
    source = row % (2 * per)
    for q in range(per):
        hit = (source == 2 * q) & (lane == 0) | (source == 2 * q + 1) & (lane == 255)
        spot = bf16(jnp.where(hit & (row < 2 * per * vectors), 1.0, 0.0))
        spots[q, 0:128] = spot
        spots[q, 128:256] = spot
    one = jnp.ones((1, 128), F32)
    lane = lanes((height, 128))
    for l in range(levels):
        coefs[0, l] = bf16(jnp.concatenate([one, sten[1, l].astype(F32)[:-1]], axis=0))
        coefs[1, l] = bf16(jnp.concatenate([sten[2, l].astype(F32)[1:], one], axis=0))
        right = jnp.dot(sten[3, l], move[:, 0:128], preferred_element_type=F32)
        left = jnp.dot(sten[4, l], move[:, 128:256], preferred_element_type=F32)
        coefs[2, l] = bf16(jnp.where(lane == 0, 1.0, right))
        coefs[3, l] = bf16(jnp.where(lane == 127, 1.0, left))
    copy.wait()


def split(x):
    high = bf16(x)
    return jnp.concatenate([high, bf16(x - high.astype(F32))], axis=1)


def final_kernel(
    dims, part, kry, adj, sten, coefs, shift, spots, cw, fwd, back, cols, mine, other,
    out_hbm, comb, low, edges, moved, out, sem,
):
    vectors, levels, fields, height = dims
    half = vectors // 2
    per = levels * fields
    total = jnp.broadcast_to(jnp.sum(part[...], axis=1, keepdims=True), (8, 128))
    mix = [jnp.broadcast_to(total[j : j + 1], (8, 128)) for j in range(vectors)]
    is_low = lax.axis_index("lev") & 1 == 0
    mine_mix = [jnp.where(is_low, mix[k], mix[half + k]) for k in range(half)]
    other_mix = [jnp.where(is_low, mix[half + k], mix[k]) for k in range(half)]

    def times(m, x):
        return (x.reshape(-1, 8, 128) * m).reshape(x.shape)

    rim_f = sum(times(mix[k], fwd[k * 16 : (k + 1) * 16]) for k in range(vectors))
    rim_b = sum(times(mix[k], back[k * 16 : (k + 1) * 16]) for k in range(vectors))
    for q in range(per):
        comb[q, 7:8] = rim_f[q : q + 1]
        comb[q, 8 + height : 9 + height] = rim_b[q : q + 1]

    lane = lanes((8, 128)) // (2 * per)
    weight = jnp.zeros((8, 128), F32)
    for k in range(vectors):
        weight = jnp.where(lane == k, mix[k], weight)
    step = 64
    for i in range(height // step):
        edges[i * step : (i + 1) * step] = split(times(weight, cols[i * step : (i + 1) * step]))

    def combine(l, f):
        for i in range(height // step):
            at = slice(i * step, (i + 1) * step)
            comb[l * fields + f, 8 + i * step : 8 + (i + 1) * step] = sum(
                times(mix[k], kry[k, l, f, at].astype(F32)) for k in range(vectors)
            )

    def column(c):
        for i in range(height // step):
            at = slice(i * step, (i + 1) * step)
            x = 0.0
            for k in range(half):
                here = slice((k * 2 + c) * height + i * step, (k * 2 + c) * height + (i + 1) * step)
                x = x + (times(mine_mix[k], mine[here]) + times(other_mix[k], other[here]))
            for l in reversed(range(levels)):
                q = l * fields + (0 if c == 0 else 3)
                x = x + comb[q, 8 + i * step : 8 + (i + 1) * step]
                low[c, l, at] = cw[c, l, at] * x

    def move(l, f):
        q = l * fields + f
        x = comb[q, 8 : 8 + height]
        moved[q % 2] = jnp.dot(split(x), shift[...], preferred_element_type=F32) + jnp.dot(
            edges[...], spots[q], preferred_element_type=F32
        )

    def stencil(l, f):
        q = l * fields + f
        for i in range(height // step):
            at = slice(i * step, (i + 1) * step)
            first = 8 + i * step
            image = (
                sten[0, l, at].astype(F32) * comb[q, first : first + step]
                + coefs[0, l, at].astype(F32) * comb[q, first - 1 : first + step - 1]
                + coefs[1, l, at].astype(F32) * comb[q, first + 1 : first + step + 1]
                + coefs[2, l, at].astype(F32) * moved[q % 2, at, 0:128]
                + coefs[3, l, at].astype(F32) * moved[q % 2, at, 128:256]
            )
            if f in (1, 4):
                image = image + low[0 if f == 1 else 1, l, at]
            out[l, f, at] = adj[l, f, at] + image

    order = [0, 3] + [f for f in range(fields) if f not in (0, 3)]
    planes = [(l, f) for f in order for l in range(levels)]
    combine(*planes[0])
    copies = []
    for n, (l, f) in enumerate(planes):
        if n + 1 < len(planes):
            combine(*planes[n + 1])
        if n == 2 * levels - 1:
            column(0)
            column(1)
        move(l, f)
        stencil(l, f)
        copy = pltpu.make_async_copy(out.at[l, f], out_hbm.at[l, f], sem.at[n])
        copy.start()
        copies.append(copy)
    for copy in copies:
        copy.wait()


def final_scratch(dims):
    _, levels, fields, height = dims
    return [
        pltpu.VMEM((levels * fields, height + 16, 128), F32),
        pltpu.VMEM((2, levels, height, 128), F32),
        pltpu.VMEM((height, 256), jnp.bfloat16),
        pltpu.VMEM((2, height, 256), F32),
        pltpu.VMEM((levels, fields, height, 128), F32),
        pltpu.SemaphoreType.DMA((levels * fields,)),
    ]


def pair_kernel(pack, got, o):
    o[...] = pack[-8:] + got[-8:]


def segment_kernel(got, mine, token, held, o):
    del token, held
    o[...] = mine[...] + got[0 : o.shape[0]]


def join_kernel(a, b, near, o):
    del near
    o[0:8] = a[...] + b[...]


def add_kernel(a, b, o):
    o[...] = a[0:8] + b[0:8]


def keep_kernel(x, token, held, o):
    del token, held
    o[...] = x[...]


def after(x, token, held):
    return local(
        keep_kernel,
        "after",
        50,
        pltpu.VMEM(x.shape, F32),
        [IN_VMEM] * 3,
        *map(pinned, (x, token, held)),
    )


def below_kernel(group_bits, got, mine, token, held, *refs):
    del token, held
    above, (send_o, mine_o) = refs[:-2], refs[-2:]
    group = lax.axis_index("lev")
    upper = group & 1 == 1
    split = mine.shape[0]
    step = 256

    def body(i, carry):
        at = pl.ds(pl.multiple_of(i * step, step), step)
        x = jnp.zeros((step, 128), F32)
        for bit, ref in zip(group_bits, above, strict=True):
            x = x + jnp.where(group & bit == 0, ref[at], 0.0)
        send_o[at] = x + jnp.where(upper, mine[at], 0.0)
        mine_o[at] = x + jnp.where(upper, 0.0, got[at])
        return carry

    lax.fori_loop(0, split // step, body, 0)


def local(kernel, name, us, out_shape, in_specs, *args, limit=SMALL, **more):
    return pl.pallas_call(
        kernel,
        out_shape=out_shape,
        in_specs=in_specs,
        out_specs=jax.tree.map(lambda _: IN_VMEM, out_shape),
        compiler_params=pltpu.CompilerParams(vmem_limit_bytes=limit),
        cost_estimate=pl.CostEstimate(
            flops=int(us * 1e9), bytes_accessed=int(us * 3.5e6), transcendentals=0
        ),
        name=name,
        **more,
    )(*args)


def add(a, b):
    return local(
        add_kernel, "add", 50, pltpu.VMEM((8, 128), F32), [IN_VMEM] * 2, pinned(a), pinned(b)
    )


def per_device(krylov, adjoint, projected, stencil, column_weight, seam_turns):
    vectors, levels, fields, height, width = krylov.shape
    dims = (vectors, levels, fields, height)
    half, per = vectors // 2, levels * fields
    tiles, groups = lax.axis_size("tile"), lax.axis_size("lev")
    count = levels * fields * height * width * tiles * groups
    total_rows = vectors * height
    bf = krylov.dtype
    dma = pltpu.SemaphoreType.DMA

    kry, pack, mine, adj = local(
        functools.partial(dots_kernel, dims, count),
        "dots",
        2,
        (
            pltpu.VMEM(krylov.shape, bf),
            pltpu.VMEM((total_rows + 8, width), F32),
            pltpu.VMEM((total_rows, width), F32),
            pltpu.VMEM(adjoint.shape, F32),
        ),
        [IN_HBM] * 3,
        *map(in_hbm, (projected, krylov, adjoint)),
        scratch_shapes=[
            pltpu.VMEM(projected.shape, F32),
            pltpu.VMEM((vectors, 8, 128), F32),
            dma((fields,)),
            dma((fields,)),
            dma,
        ],
    )
    sten, near, far, cols = local(
        functools.partial(strips_kernel, dims),
        "strips",
        1.5,
        (
            pltpu.VMEM(stencil.shape, bf),
            pltpu.VMEM((vectors * 16 + 8, width), F32),
            pltpu.VMEM((vectors * 16, width), F32),
            pltpu.VMEM((height, width), F32),
        ),
        [IN_VMEM, IN_HBM],
        pinned(kry),
        in_hbm(stencil),
        scratch_shapes=[dma],
    )

    first = exchange(pack, "lev", 1)
    part = local(
        pair_kernel, "pair", 0.1, pltpu.VMEM((8, width), F32), [IN_VMEM] * 2, pinned(pack), pinned(first)
    )
    segment = local(
        segment_kernel,
        "segment",
        50,
        pltpu.VMEM(mine.shape, F32),
        [IN_VMEM] * 4,
        *map(pinned, (first, mine, part, kry)),
    )
    above = []
    for bit in bits("lev")[1:]:
        if above:
            segment = segment + above[-1]
        above.append(exchange(segment, "lev", bit))
    cols = after(cols, part, kry)
    up = shifted(cols, "tile", STRIDE)
    down = up if (2 * STRIDE) % tiles == 0 else shifted(cols, "tile", -STRIDE)

    for bit in bits("lev")[1:-1]:
        part = add(part, exchange(part, "lev", bit))
    got = exchange(part, "lev", bits("lev")[-1])
    near = local(
        join_kernel,
        "join",
        50,
        pltpu.VMEM(near.shape, F32),
        [IN_VMEM] * 3,
        *map(pinned, (part, got, near)),
        input_output_aliases={2: 0},
    )
    far = after(far, near, kry)
    got = exchange(near, "tile", 1)
    part = add(near, got)
    near = got
    far = lax.ppermute(
        far, "tile", [(i, (i + 1 if i % 2 else i - 1) % tiles) for i in range(tiles)]
    )
    for bit in bits("tile")[1:-1]:
        part = add(part, exchange(part, "tile", bit))
    token = part
    for bit in bits("tile")[-1:]:
        part = add(part, exchange(part, "tile", bit))

    send, mine = local(
        functools.partial(below_kernel, bits("lev")[1:]),
        "below",
        50,
        (pltpu.VMEM(mine.shape, F32), pltpu.VMEM(mine.shape, F32)),
        [IN_VMEM] * (4 + len(above)),
        *map(pinned, (first, mine, token, kry, *above)),
    )
    other = exchange(send, "lev", 1)

    coefs, shift, spots, cw = local(
        functools.partial(tables_kernel, dims),
        "tables",
        1.5,
        (
            pltpu.VMEM((4,) + stencil.shape[1:], bf),
            pltpu.VMEM((256, 256), bf),
            pltpu.VMEM((per, 256, 256), bf),
            pltpu.VMEM(column_weight.shape, F32),
        ),
        [IN_VMEM, IN_HBM, IN_VMEM],
        pinned(sten),
        in_hbm(column_weight),
        pinned(token),
        scratch_shapes=[dma],
    )
    fwd, back, cols = local(
        functools.partial(turn_kernel, dims),
        "turn",
        1,
        (
            pltpu.VMEM(far.shape, F32),
            pltpu.VMEM(far.shape, F32),
            pltpu.VMEM(cols.shape, F32),
        ),
        [IN_VMEM] * 5,
        *map(pinned, (seam_turns, near, far, up, down)),
    )

    return pl.pallas_call(
        functools.partial(final_kernel, dims),
        out_shape=jax.ShapeDtypeStruct(adjoint.shape, F32),
        in_specs=[IN_VMEM] * 13,
        out_specs=IN_HBM,
        scratch_shapes=final_scratch(dims),
        compiler_params=pltpu.CompilerParams(vmem_limit_bytes=LARGE),
        name="final",
    )(
        *map(
            pinned,
            (part, kry, adj, sten, coefs, shift, spots, cw, fwd, back, cols, mine, other),
        )
    )


def solution(mesh):
    placed = (
        P(None, "lev", None, "tile", None),
        P("lev", None, "tile", None),
        P(),
        P(None, "lev", "tile", None),
        P(None, "lev", "tile", None),
        P("tile", None),
    )
    return jax.shard_map(
        per_device,
        mesh=mesh,
        in_specs=placed,
        out_specs=P("lev", None, "tile", None),
        check_vma=False,
    )
```

time: 158 us -> 29.4 us (0.19)
  blocking collectives: 40.3 us -> 0 us
  other arithmetic: 38.6 us -> 0 us
  local copies, waits for them, and re-layouts: 38 us -> 0.71 us
  between operations: 31.4 us -> 0.09 us
  Pallas kernels: 0 us -> 13.1 us
  starting transfers between devices: 8.9 us -> 13 us
  waiting for transfers between devices: 0.03 us -> 2.17 us
    psum x1 -> x0, blocking collectives: 40.3 us -> none  [per_device(): coupling = lax.psum(partial_value, ('tile', 'lev')) / count]
    slice x12 -> x0, local copies, waits for them, and re-layouts: 24.7 us -> none  [the longest x2 9.72 us: apply_operator(): up_strip = shifted(plus_cols[..., -1], 'tile', STRIDE)]
    reduce_sum x4 -> x0, other arithmetic: 24.5 us -> none  [the longest x1 11.2 us: per_device(): partial_value = jnp.sum(vectors * adjoint[None], axis=(1, 2, 3, 4))]
    pallas_call x0 -> x14, Pallas kernels: none -> 13.1 us  [the longest x13 10.5 us: local(): pl.pallas_call(kernel, out_shape=out_shape, in_specs=in_specs, out_specs=...]
    select_n x8 -> x0, other arithmetic: 6.42 us -> none  [the longest x4 6.34 us: step(): return jnp.where(reached, new, before)]
    broadcast_in_dim x4 -> x0, local copies, waits for them, and re-layouts: 6.3 us -> none  [the longest x1 3.19 us: apply_operator(): down_strip[..., None]]
    ppermute x4 -> x9, starting transfers between devices: 8.89 us -> 13 us  [the longest x7 7.8 us: exchange(): return lax.ppermute(x, axis, [(i, i ^ bit) for i in range(size)])]
    another operation x1 -> x0, other arithmetic: 3.24 us -> none  [apply_operator(): suffix = jnp.cumsum(carried[:, ::-1], axis=1)[:, ::-1] + below[:, None]]
  transfers between devices with their start and end apart: 5 -> 9, of which waited for: 0 -> 4; matrix products, arithmetic and copies ran while one was open for 32% -> 0% of each run, Pallas kernels for 0% -> 25%
where the time goes in v2:
time: 29.4 us; the launch traced here: 29.1 us
  Pallas kernels  13.1 us (45%)
  starting transfers between devices  13 us (44%)
  waiting for transfers between devices  2.17 us (7%)
  local copies, waits for them, and re-layouts  0.71 us (2%)
    pallas_call x13, Pallas kernels, local(): pl.pallas_call(kernel, out_shape=out_shape, in_specs=in_specs, out_specs=...  10.5 us
    ppermute x7, starting transfers between devices, exchange(): return lax.ppermute(x, axis, [(i, i ^ bit) for i in range(size)])  7.8 us
    ppermute x1, starting transfers between devices, per_device(): lax.ppermute(far, 'tile', [(i, (i + 1 if i % 2 else i - 1) % tiles) for i...  2.63 us
    pallas_call x1, Pallas kernels, per_device(): pl.pallas_call(functools.partial(final_kernel, dims), out_shape=jax.Shape...  2.62 us
    ppermute x1, starting transfers between devices, shifted(): return lax.ppermute(x, axis, [(i, (i + steps) % size) for i in range(size)])  2.59 us
    ppermute x7, waiting for transfers between devices, exchange(): return lax.ppermute(x, axis, [(i, i ^ bit) for i in range(size)])  2.17 us
    unnamed x10, local copies, waits for them, and re-layouts  0.71 us
  transfers between devices with their start and end apart: 9, of which 4 were waited for; matrix products, arithmetic and copies ran while one was open for 0% of the time, Pallas kernels for 25%

profile of v2, /device:TPU:0, one launch (start us, length us, event | category | flops | bytes accessed | tf_op | source)
XLA Modules:
  0.0 29.1 jit_solution(8013462640763255771)
XLA Ops:
  0.0 3.1 %dots.1 = (bf16[4,2,5,256,128]{4,3,2,1,0:T(8,128)(2,1)S(1)}, f32[1032,128]{1,0:T(8,128)S(1)}, f32[1024,128]{1,0:T(8,128)S(1)}, f32[2,5,256,128]{3,2,1,0:T(8,128)S(1)}) custom-call(f32[4,4]{1,0:T(4,128)} %projected.1, bf16[4,2,5,256,128]{4,3,2,1,0:T(8,128)(2,1)} %kry.1, f32[2,5,256,128]{3,2,1,0:T(8,128)} %adj.1), custom_call_target="tpu_custom_call" | custom-call | flops 2000000000 | bytes 7000000 | tf_op jit(solution)/shard_map/dots/pallas_call | solution.py:402
  3.1 0.6 %collective-permute-start = (f32[1032,128]{1,0:T(8,128)S(1)}, f32[1032,128]{1,0:T(8,128)S(1)}, u32[]{:S(2)}, u32[]{:S(2)}) collective-permute-start(f32[1032,128]{1,0:T(8,128)S(1)} %get-tuple-element.22.pack), channel_id=1, source_target_pairs={{0,1},{1,0},{2,3},{3,2},{4,5},{5,4},{6,7},{7,6},{8,9},{9,8},{10,11... | collective-permute-start | bytes 1585160 | tf_op jit(solution)/shard_map/ppermute | solution.py:29
  3.6 1.4 %strips.1 = (bf16[5,2,256,128]{3,2,1,0:T(8,128)(2,1)S(1)}, f32[72,128]{1,0:T(8,128)S(1)}, f32[64,128]{1,0:T(8,128)S(1)}, f32[256,128]{1,0:T(8,128)S(1)}) custom-call(bf16[4,2,5,256,128]{4,3,2,1,0:T(8,128)(2,1)S(1)} %get-tuple-element.23.kry_v.held.kry, bf16[5,2,256,128]{3,2,1,0:T(8,128)(2,1)} %sten.1), custom_call_target="tpu_custom_call" | custom-call | flops 1500000000 | bytes 5250000 | tf_op jit(solution)/shard_map/strips/pallas_call | solution.py:402
  5.1 0.1 collective-permute-done.got
  5.2 0.0 copy-start
  5.2 2.8 %collective-permute-start.1 = (f32[8,128]{1,0:T(8,128)S(1)}, f32[8,128]{1,0:T(8,128)S(1)}, u32[]{:S(2)}, u32[]{:S(2)}) collective-permute-start(f32[8,128]{1,0:T(8,128)S(1)} %pair.1.a.token), channel_id=1, source_target_pairs={{0,2},{1,3},{2,0},{3,1},{4,6},{5,7},{6,4},{7,5},{8,10},{9,11},{10,... | collective-permute-start | bytes 12296 | tf_op jit(solution)/shard_map/ppermute | solution.py:29
  8.0 0.9 %segment.1 = f32[1024,128]{1,0:T(8,128)} custom-call(f32[1032,128]{1,0:T(8,128)S(1)} %collective-permute-done.got, f32[1024,128]{1,0:T(8,128)S(1)} %get-tuple-element.36.mine, f32[8,128]{1,0:T(8,128)S(1)} %pair.1.a.token, bf16[4,2,5,256,128]{4,3,2,1,0:T(8,128)(2,1)S(1)} %get-tuple-element.23.kry_v.held.kry), custom_call_target="tpu_custom_call" | custom-call | flops 49999998976 | bytes 175000000 | tf_op jit(solution)/shard_map/segment/pallas_call | solution.py:402
  8.9 0.0 copy-done
  8.9 0.1 collective-permute-start.7
  9.0 0.6 %collective-permute-done.1.b = f32[8,128]{1,0:T(8,128)S(1)} collective-permute-done((f32[8,128]{1,0:T(8,128)S(1)}, f32[8,128]{1,0:T(8,128)S(1)}, u32[]{:S(2)}, u32[]{:S(2)}) %collective-permute-start.1) | collective-permute-done | bytes 4128 | tf_op jit(solution)/shard_map/ppermute | solution.py:29
  9.6 2.0 %collective-permute-start.2 = (f32[72,128]{1,0:T(8,128)S(1)}, f32[72,128]{1,0:T(8,128)S(1)}, u32[]{:S(2)}, u32[]{:S(2)}) collective-permute-start(f32[72,128]{1,0:T(8,128)S(1)} %join.1.a.token), channel_id=1, source_target_pairs={{0,4},{4,0},{8,12},{12,8},{16,20},{20,16},{24,28},{28,24},{1,5},{5... | collective-permute-start | bytes 110600 | tf_op jit(solution)/shard_map/ppermute | solution.py:29
  11.6 0.6 %after.3 = f32[256,128]{1,0:T(8,128)} custom-call(f32[256,128]{1,0:T(8,128)S(1)} %get-tuple-element.32.x, f32[8,128]{1,0:T(8,128)S(1)} %pair.1.a.token, bf16[4,2,5,256,128]{4,3,2,1,0:T(8,128)(2,1)S(1)} %get-tuple-element.23.kry_v.held.kry), custom_call_target="tpu_custom_call" | custom-call | flops 49999998976 | bytes 175000000 | tf_op jit(solution)/shard_map/after/pallas_call | solution.py:402
  12.2 2.6 %collective-permute-start.6 = (f32[256,128]{1,0:T(8,128)}, f32[256,128]{1,0:T(8,128)}, u32[]{:S(2)}, u32[]{:S(2)}) collective-permute-start(f32[256,128]{1,0:T(8,128)} %after.3), channel_id=1, source_target_pairs={{0,16},{4,20},{8,24},{12,28},{16,0},{20,4},{24,8},{28,12},{1,17},{... | collective-permute-start | bytes 393224 | tf_op jit(solution)/shard_map/ppermute | solution.py:34
  14.8 0.0 collective-permute-done.2.b.near
  14.8 0.0 copy-start.2
  14.8 0.6 %copy-done.2 = f32[72,128]{1,0:T(8,128)} copy-done((f32[72,128]{1,0:T(8,128)}, f32[72,128]{1,0:T(8,128)S(1)}, u32[]{:S(2)}) %copy-start.2) | copy-done | bytes 36888
  15.4 1.6 %collective-permute-start.3 = (f32[8,128]{1,0:T(8,128)S(1)}, f32[8,128]{1,0:T(8,128)S(1)}, u32[]{:S(2)}, u32[]{:S(2)}) collective-permute-start(f32[8,128]{1,0:T(8,128)S(1)} %add.3.a), channel_id=1, source_target_pairs={{0,8},{4,12},{8,0},{12,4},{16,24},{20,28},{24,16},{28,20},{1,9},{5... | collective-permute-start | bytes 12296 | tf_op jit(solution)/shard_map/ppermute | solution.py:29
  17.0 0.6 %after.2 = f32[64,128]{1,0:T(8,128)} custom-call(f32[64,128]{1,0:T(8,128)S(1)} %get-tuple-element.31.x, f32[72,128]{1,0:T(8,128)S(1)} %join.1.a.token, bf16[4,2,5,256,128]{4,3,2,1,0:T(8,128)(2,1)S(1)} %get-tuple-element.23.kry_v.held.kry), custom_call_target="tpu_custom_call" | custom-call | flops 49999998976 | bytes 175000000 | tf_op jit(solution)/shard_map/after/pallas_call | solution.py:402
  17.6 2.6 %collective-permute-start.5 = (f32[64,128]{1,0:T(8,128)}, f32[64,128]{1,0:T(8,128)}, u32[]{:S(2)}, u32[]{:S(2)}) collective-permute-start(f32[64,128]{1,0:T(8,128)} %after.2), channel_id=1, source_target_pairs={{0,28},{4,8},{8,4},{12,16},{16,12},{20,24},{24,20},{28,0},{1,29},{... | collective-permute-start | bytes 98312 | tf_op jit(solution)/shard_map/ppermute | solution.py:505
  20.3 0.0 collective-permute-done.3.b
  20.3 0.7 %collective-permute-start.4 = (f32[8,128]{1,0:T(8,128)S(1)}, f32[8,128]{1,0:T(8,128)S(1)}, u32[]{:S(2)}, u32[]{:S(2)}) collective-permute-start(f32[8,128]{1,0:T(8,128)S(1)} %add.4.a.token), channel_id=1, source_target_pairs={{0,16},{4,20},{8,24},{12,28},{16,0},{20,4},{24,8},{28,12},{1,17},{... | collective-permute-start | bytes 12296 | tf_op jit(solution)/shard_map/ppermute | solution.py:29
  20.9 0.0 copy-start.1
  20.9 1.1 %tables.1 = (bf16[4,2,256,128]{3,2,1,0:T(8,128)(2,1)S(1)}, bf16[256,256]{1,0:T(8,128)(2,1)S(1)}, bf16[10,256,256]{2,1,0:T(8,128)(2,1)S(1)}, f32[2,2,256,128]{3,2,1,0:T(8,128)S(1)}) custom-call(bf16[5,2,256,128]{3,2,1,0:T(8,128)(2,1)S(1)} %get-tuple-element.26.sten, f32[2,2,256,128]{3,2,1,0:T(8,128)} %cw.1, f32[8,128]{1,0:T(8,128)S(1)} %add.4.a.token), custom_call_target="tpu_custom_call" | custom-call | flops 1500000000 | bytes 5250000 | tf_op jit(solution)/shard_map/tables/pallas_call | solution.py:402
  22.0 0.8 %collective-permute-done.7.refs_0_ = f32[1024,128]{1,0:T(8,128)} collective-permute-done((f32[1024,128]{1,0:T(8,128)}, f32[1024,128]{1,0:T(8,128)}, u32[]{:S(2)}, u32[]{:S(2)}) %collective-permute-start.7) | collective-permute-done | bytes 524320 | tf_op jit(solution)/shard_map/ppermute | solution.py:29
  22.9 0.0 copy-done.1
  22.9 1.2 %below.1 = (f32[1024,128]{1,0:T(8,128)S(1)}, f32[1024,128]{1,0:T(8,128)S(1)}) custom-call(f32[1032,128]{1,0:T(8,128)S(1)} %copy-done.1, f32[1024,128]{1,0:T(8,128)S(1)} %get-tuple-element.36.mine, f32[8,128]{1,0:T(8,128)S(1)} %add.4.a.token, bf16[4,2,5,256,128]{4,3,2,1,0:T(8,128)(2,1)S(1)} %get-tuple-element.23.kry_v.held.kry, ...), custom_call_target="tpu_custom_call" | custom-call | flops 49999998976 | bytes 175000000 | tf_op jit(solution)/shard_map/below/pallas_call | solution.py:402
  24.1 0.0 copy-start.3
  24.1 0.0 copy-start.4
  24.1 0.1 collective-permute-start.8
  24.2 0.6 %collective-permute-done.4.b = f32[8,128]{1,0:T(8,128)S(1)} collective-permute-done((f32[8,128]{1,0:T(8,128)S(1)}, f32[8,128]{1,0:T(8,128)S(1)}, u32[]{:S(2)}, u32[]{:S(2)}) %collective-permute-start.4) | collective-permute-done | bytes 4128 | tf_op jit(solution)/shard_map/ppermute | solution.py:29
  24.8 0.0 collective-permute-done.5.far
  24.8 0.0 collective-permute-done.6.up.down
  24.8 0.1 copy-done.3
  24.9 0.0 copy-done.4
  24.9 1.5 %turn.1 = (f32[64,128]{1,0:T(8,128)S(1)}, f32[64,128]{1,0:T(8,128)S(1)}, f32[256,128]{1,0:T(8,128)S(1)}) custom-call(s32[1,4]{1,0:T(1,128)S(1)} %copy-done.4, f32[72,128]{1,0:T(8,128)S(1)} %copy-done.3, f32[64,128]{1,0:T(8,128)} %collective-permute-done.5.far, f32[256,128]{1,0:T(8,128)} %collective-permute-done.6.up.down, ...), custom_call_target="tpu_custom_call" | custom-call | flops 1000000000 | bytes 3500000 | tf_op jit(solution)/shard_map/turn/pallas_call | solution.py:402
  26.4 0.0 collective-permute-done.8.other
  26.4 2.6 %final.1 = f32[2,5,256,128]{3,2,1,0:T(8,128)} custom-call(f32[8,128]{1,0:T(8,128)S(1)} %add.5.part, bf16[4,2,5,256,128]{4,3,2,1,0:T(8,128)(2,1)S(1)} %get-tuple-element.23.kry_v.held.kry, f32[2,5,256,128]{3,2,1,0:T(8,128)S(1)} %get-tuple-element.25.adj, bf16[5,2,256,128]{3,2,1,0:T(8,128)(2,1)S(1)} %get-tuple-element.26.sten, ...), custom_call_target="tpu_custom_call" | custom-call | tf_op jit(solution)/shard_map/final/pallas_call | solution.py:553
  (5 shorter events, 0.0 us)
Async XLA Ops:
  3.1 2.1 %collective-permute-start = (f32[1032,128]{1,0:T(8,128)S(1)}, f32[1032,128]{1,0:T(8,128)S(1)}, u32[]{:S(2)}, u32[]{:S(2)}) collective-permute-start(f32[1032,128]{1,0:T(8,128)S(1)} %get-tuple-element.22.pack), channel_id=1, source_target_pairs={{0,1},{1,0},{2,3},{3,2},{4,5},{5,4},{6,7},{7,6},{8,9},{9,8},{10,11... | collective-permute-start | bytes 1585160 | tf_op jit(solution)/shard_map/ppermute | solution.py:29
  5.2 3.7 %copy-start = (f32[1032,128]{1,0:T(8,128)}, f32[1032,128]{1,0:T(8,128)S(1)}, u32[]{:S(2)}) copy-start(f32[1032,128]{1,0:T(8,128)S(1)} %collective-permute-done.got) | copy-start | bytes 1585156
  5.2 4.4 %collective-permute-start.1 = (f32[8,128]{1,0:T(8,128)S(1)}, f32[8,128]{1,0:T(8,128)S(1)}, u32[]{:S(2)}, u32[]{:S(2)}) collective-permute-start(f32[8,128]{1,0:T(8,128)S(1)} %pair.1.a.token), channel_id=1, source_target_pairs={{0,2},{1,3},{2,0},{3,1},{4,6},{5,7},{6,4},{7,5},{8,10},{9,11},{10,... | collective-permute-start | bytes 12296 | tf_op jit(solution)/shard_map/ppermute | solution.py:29
  8.9 14.0 %collective-permute-start.7 = (f32[1024,128]{1,0:T(8,128)}, f32[1024,128]{1,0:T(8,128)}, u32[]{:S(2)}, u32[]{:S(2)}) collective-permute-start(f32[1024,128]{1,0:T(8,128)} %segment.1), channel_id=1, source_target_pairs={{0,2},{1,3},{2,0},{3,1},{4,6},{5,7},{6,4},{7,5},{8,10},{9,11},{10,... | collective-permute-start | bytes 1572872 | tf_op jit(solution)/shard_map/ppermute | solution.py:29
  9.6 5.2 %collective-permute-start.2 = (f32[72,128]{1,0:T(8,128)S(1)}, f32[72,128]{1,0:T(8,128)S(1)}, u32[]{:S(2)}, u32[]{:S(2)}) collective-permute-start(f32[72,128]{1,0:T(8,128)S(1)} %join.1.a.token), channel_id=1, source_target_pairs={{0,4},{4,0},{8,12},{12,8},{16,20},{20,16},{24,28},{28,24},{1,5},{5... | collective-permute-start | bytes 110600 | tf_op jit(solution)/shard_map/ppermute | solution.py:29
  12.2 12.5 %collective-permute-start.6 = (f32[256,128]{1,0:T(8,128)}, f32[256,128]{1,0:T(8,128)}, u32[]{:S(2)}, u32[]{:S(2)}) collective-permute-start(f32[256,128]{1,0:T(8,128)} %after.3), channel_id=1, source_target_pairs={{0,16},{4,20},{8,24},{12,28},{16,0},{20,4},{24,8},{28,12},{1,17},{... | collective-permute-start | bytes 393224 | tf_op jit(solution)/shard_map/ppermute | solution.py:34
  14.8 0.6 %copy-start.2 = (f32[72,128]{1,0:T(8,128)}, f32[72,128]{1,0:T(8,128)S(1)}, u32[]{:S(2)}) copy-start(f32[72,128]{1,0:T(8,128)S(1)} %collective-permute-done.2.b.near) | copy-start | bytes 110596
  15.4 4.8 %collective-permute-start.3 = (f32[8,128]{1,0:T(8,128)S(1)}, f32[8,128]{1,0:T(8,128)S(1)}, u32[]{:S(2)}, u32[]{:S(2)}) collective-permute-start(f32[8,128]{1,0:T(8,128)S(1)} %add.3.a), channel_id=1, source_target_pairs={{0,8},{4,12},{8,0},{12,4},{16,24},{20,28},{24,16},{28,20},{1,9},{5... | collective-permute-start | bytes 12296 | tf_op jit(solution)/shard_map/ppermute | solution.py:29
  17.6 7.2 %collective-permute-start.5 = (f32[64,128]{1,0:T(8,128)}, f32[64,128]{1,0:T(8,128)}, u32[]{:S(2)}, u32[]{:S(2)}) collective-permute-start(f32[64,128]{1,0:T(8,128)} %after.2), channel_id=1, source_target_pairs={{0,28},{4,8},{8,4},{12,16},{16,12},{20,24},{24,20},{28,0},{1,29},{... | collective-permute-start | bytes 98312 | tf_op jit(solution)/shard_map/ppermute | solution.py:505
  20.3 4.5 %collective-permute-start.4 = (f32[8,128]{1,0:T(8,128)S(1)}, f32[8,128]{1,0:T(8,128)S(1)}, u32[]{:S(2)}, u32[]{:S(2)}) collective-permute-start(f32[8,128]{1,0:T(8,128)S(1)} %add.4.a.token), channel_id=1, source_target_pairs={{0,16},{4,20},{8,24},{12,28},{16,0},{20,4},{24,8},{28,12},{1,17},{... | collective-permute-start | bytes 12296 | tf_op jit(solution)/shard_map/ppermute | solution.py:29
  20.9 2.0 %copy-start.1 = (f32[1032,128]{1,0:T(8,128)S(1)}, f32[1032,128]{1,0:T(8,128)}, u32[]{:S(2)}) copy-start(f32[1032,128]{1,0:T(8,128)} %copy-done) | copy-start | bytes 1585156
  24.1 0.8 %copy-start.3 = (f32[72,128]{1,0:T(8,128)S(1)}, f32[72,128]{1,0:T(8,128)}, u32[]{:S(2)}) copy-start(f32[72,128]{1,0:T(8,128)} %copy-done.2) | copy-start | bytes 110596
  24.1 0.8 %copy-start.4 = (s32[1,4]{1,0:T(1,128)S(1)}, s32[1,4]{1,0:T(1,128)}, u32[]{:S(2)}) copy-start(s32[1,4]{1,0:T(1,128)} %turns.1) | copy-start | bytes 52
  24.1 2.3 %collective-permute-start.8 = (f32[1024,128]{1,0:T(8,128)S(1)}, f32[1024,128]{1,0:T(8,128)S(1)}, u32[]{:S(2)}, u32[]{:S(2)}) collective-permute-start(f32[1024,128]{1,0:T(8,128)S(1)} %get-tuple-element.38), channel_id=1, source_target_pairs={{0,1},{1,0},{2,3},{3,2},{4,5},{5,4},{6,7},{7,6},{8,9},{9,8},{10,11... | collective-permute-start | bytes 1572872 | tf_op jit(solution)/shard_map/ppermute | solution.py:29

commit v3 on v2

--- a/solution.py
+++ b/solution.py
@@ -49,6 +49,11 @@
 
 def bf16(x):
     return x.astype(jnp.bfloat16)
+
+
+def split(x):
+    high = bf16(x)
+    return jnp.concatenate([high, bf16(x - high.astype(F32))], axis=1)
 
 
 def ends_to(last, first):
@@ -75,6 +80,31 @@
         )
         for copy in copies[f]:
             copy.start()
+    step = 128
+    accs = [jnp.zeros((8, 128), F32) for _ in range(vectors)]
+    for f in order:
+        for copy in copies[f]:
+            copy.wait()
+        for l in range(levels):
+
+            def body(i, accs, f=f, l=l):
+                start = pl.multiple_of(i * step, step)
+                at = pl.ds(start, step)
+                y = adj_v[l, f, at]
+                xs = [kry_v[k, l, f, at].astype(F32) for k in range(vectors)]
+                if f in (0, 3):
+                    for k in range(half):
+                        to = pl.ds(start + (k * 2 + (0 if f == 0 else 1)) * height, step)
+                        a, b = xs[k], xs[half + k]
+                        for ref, x in ((mine, jnp.where(upper, b, a)), (pack, jnp.where(upper, a, b))):
+                            ref[to] = x if l == 0 else ref[to] + x
+                out = [
+                    acc + jnp.sum((x * y).reshape(step // 8, 8, 128), axis=0)
+                    for acc, x in zip(accs, xs, strict=True)
+                ]
+                return out
+
+            accs = lax.fori_loop(0, height // step, body, accs)
     copy_p.wait()
     r = rows((8, 128))
     for k in range(vectors):
@@ -82,45 +112,13 @@
         for j in range(vectors):
             m = jnp.where(r == j, proj_v[k : k + 1, j : j + 1] * (0.5 / count), m)
         mixer[k] = m
-    step = 128
-    accs = [jnp.zeros((8, 128), F32) for _ in range(vectors)]
-    for f in order:
-        for copy in copies[f]:
-            copy.wait()
-        for l in range(levels):
-
-            def body(i, accs, f=f, l=l):
-                start = pl.multiple_of(i * step, step)
-                at = pl.ds(start, step)
-                y = adj_v[l, f, at]
-                out = []
-                for k in range(vectors):
-                    x = kry_v[k, l, f, at].astype(F32)
-                    if f in (0, 3):
-                        c = 0 if f == 0 else 1
-                        to = pl.ds(start + ((k % half) * 2 + c) * height, step)
-
-                        def put(ref, x=x, to=to):
-                            if l == 0:
-                                ref[to] = x
-                            else:
-                                ref[to] = ref[to] + x
-
-                        first, second = (mine, pack) if k < half else (pack, mine)
-                        pl.when(jnp.logical_not(upper))(functools.partial(put, first))
-                        pl.when(upper)(functools.partial(put, second))
-                    p = x * y
-                    out.append(accs[k] + jnp.sum(p.reshape(step // 8, 8, 128), axis=0))
-                return out
-
-            accs = lax.fori_loop(0, height // step, body, accs)
     total = jnp.zeros((8, 128), F32)
     for k in range(vectors):
         total = total + mixer[k] * jnp.sum(accs[k], axis=0, keepdims=True)
     pack[vectors * height : vectors * height + 8] = total
 
 
-def strips_kernel(dims, kry_v, sten, sten_v, near, far, cols, sem):
+def strips_kernel(dims, kry_v, sten, sten_v, near, far, cols_t, cols, sem):
     vectors, levels, fields, height = dims
     per = levels * fields
     even_tile = lax.axis_index("tile") & 1 == 0
@@ -163,7 +161,7 @@
         jnp.concatenate(weights, axis=0),
         preferred_element_type=F32,
     )
-    cols[...] = cols[...] * coeff
+    cols_t[...] = jnp.transpose(cols[...] * coeff)[0 : cols_t.shape[0]]
 
 
 def turn_of(r):
@@ -176,7 +174,8 @@
     vectors, levels, fields, height = dims
     per = levels * fields
     n = vectors * 16
-    flip = (lanes((128, 128)) + rows((128, 128)) == 127).astype(F32)
+    flip = bf16(jnp.where(lanes((128, 128)) + rows((128, 128)) == 127, 1.0, 0.0))
+    flip = jnp.concatenate([flip, flip], axis=0)
     r = rows((n, 128)) % 16
     field = r % fields
     real = r < per
@@ -187,25 +186,31 @@
         x = jnp.where(even_tile, first, second)
         x = jnp.where(
             turning % 2 == 1,
-            jnp.dot(x, flip, precision=lax.Precision.HIGHEST, preferred_element_type=F32),
+            jnp.dot(split(x), flip, preferred_element_type=F32),
             x,
         )
         cosine, sine = turn_of(turning)
         u = cosine * x - sine * pltpu.roll(x, n - 1, 0)
         v = sine * pltpu.roll(x, 1, 0) + cosine * x
         out[...] = jnp.where(real & (field == 2), u, jnp.where(real & (field == 3), v, x))
-    lane = lanes((height, 128))
-    even = lane % 2 == 0
+    strips = up.shape[0]
+    r = rows((strips, 1))
+    even = r % 2 == 0
     x = jnp.where(even, up[...], down[...])
-    mirror = (lanes((height, height)) + rows((height, height)) == height - 1).astype(F32)
-    mirrored = jnp.dot(mirror, x, precision=lax.Precision.HIGHEST, preferred_element_type=F32)
-    turning = jnp.where(lanes((1, 128)) % 2 == 0, turns[0:1, 2:3], turns[0:1, 3:4])
+    mirror = bf16(jnp.where(lanes((height, height)) + rows((height, height)) == height - 1, 1.0, 0.0))
+    mirrored = jnp.dot(
+        split(x), jnp.concatenate([mirror, mirror], axis=0), preferred_element_type=F32
+    )
+    turning = jnp.where(even, turns[0:1, 2:3], turns[0:1, 3:4])
     x = jnp.where(turning % 2 == 1, mirrored, x)
     cosine, sine = turn_of(turning)
-    field = lane % (2 * fields) // 2
-    u = cosine * x - sine * pltpu.roll(x, 126, 1)
-    v = sine * pltpu.roll(x, 2, 1) + cosine * x
-    cols_o[...] = jnp.where(field == 2, u, jnp.where(field == 3, v, x))
+    field = r % (2 * fields) // 2
+    u = cosine * x - sine * pltpu.roll(x, strips - 2, 0)
+    v = sine * pltpu.roll(x, 2, 0) + cosine * x
+    x = jnp.where(field == 2, u, jnp.where(field == 3, v, x))
+    cols_o[...] = jnp.transpose(
+        jnp.concatenate([x, jnp.zeros((128 - strips, height), F32)], axis=0)
+    )
 
 
 def tables_kernel(dims, sten, cw, token, coefs, shift, spots, cw_v, sem):
@@ -236,11 +241,6 @@
     copy.wait()
 
 
-def split(x):
-    high = bf16(x)
-    return jnp.concatenate([high, bf16(x - high.astype(F32))], axis=1)
-
-
 def final_kernel(
     dims, part, kry, adj, sten, coefs, shift, spots, cw, fwd, back, cols, mine, other,
     out_hbm, comb, low, edges, moved, out, sem,
@@ -353,12 +353,13 @@
     o[...] = mine[...] + got[0 : o.shape[0]]
 
 
-def join_kernel(a, b, near, o):
-    del near
+def join_kernel(a, b, near, held, o):
+    del near, held
     o[0:8] = a[...] + b[...]
 
 
-def add_kernel(a, b, o):
+def add_kernel(a, b, *rest):
+    o = rest[-1]
     o[...] = a[0:8] + b[0:8]
 
 
@@ -371,7 +372,7 @@
     return local(
         keep_kernel,
         "after",
-        50,
+        12,
         pltpu.VMEM(x.shape, F32),
         [IN_VMEM] * 3,
         *map(pinned, (x, token, held)),
@@ -413,9 +414,10 @@
     )(*args)
 
 
-def add(a, b):
+def add(a, b, *held):
     return local(
-        add_kernel, "add", 50, pltpu.VMEM((8, 128), F32), [IN_VMEM] * 2, pinned(a), pinned(b)
+        add_kernel, "add", 12, pltpu.VMEM((8, 128), F32), [IN_VMEM] * (2 + len(held)),
+        *map(pinned, (a, b, *held)),
     )
 
 
@@ -457,12 +459,12 @@
             pltpu.VMEM(stencil.shape, bf),
             pltpu.VMEM((vectors * 16 + 8, width), F32),
             pltpu.VMEM((vectors * 16, width), F32),
-            pltpu.VMEM((height, width), F32),
+            pltpu.VMEM((2 * vectors * per, height), F32),
         ),
         [IN_VMEM, IN_HBM],
         pinned(kry),
         in_hbm(stencil),
-        scratch_shapes=[dma],
+        scratch_shapes=[pltpu.VMEM((height, width), F32), dma],
     )
 
     first = exchange(pack, "lev", 1)
@@ -472,7 +474,7 @@
     segment = local(
         segment_kernel,
         "segment",
-        50,
+        12,
         pltpu.VMEM(mine.shape, F32),
         [IN_VMEM] * 4,
         *map(pinned, (first, mine, part, kry)),
@@ -488,39 +490,6 @@
 
     for bit in bits("lev")[1:-1]:
         part = add(part, exchange(part, "lev", bit))
-    got = exchange(part, "lev", bits("lev")[-1])
-    near = local(
-        join_kernel,
-        "join",
-        50,
-        pltpu.VMEM(near.shape, F32),
-        [IN_VMEM] * 3,
-        *map(pinned, (part, got, near)),
-        input_output_aliases={2: 0},
-    )
-    far = after(far, near, kry)
-    got = exchange(near, "tile", 1)
-    part = add(near, got)
-    near = got
-    far = lax.ppermute(
-        far, "tile", [(i, (i + 1 if i % 2 else i - 1) % tiles) for i in range(tiles)]
-    )
-    for bit in bits("tile")[1:-1]:
-        part = add(part, exchange(part, "tile", bit))
-    token = part
-    for bit in bits("tile")[-1:]:
-        part = add(part, exchange(part, "tile", bit))
-
-    send, mine = local(
-        functools.partial(below_kernel, bits("lev")[1:]),
-        "below",
-        50,
-        (pltpu.VMEM(mine.shape, F32), pltpu.VMEM(mine.shape, F32)),
-        [IN_VMEM] * (4 + len(above)),
-        *map(pinned, (first, mine, token, kry, *above)),
-    )
-    other = exchange(send, "lev", 1)
-
     coefs, shift, spots, cw = local(
         functools.partial(tables_kernel, dims),
         "tables",
@@ -534,9 +503,39 @@
         [IN_VMEM, IN_HBM, IN_VMEM],
         pinned(sten),
         in_hbm(column_weight),
-        pinned(token),
+        pinned(part),
         scratch_shapes=[dma],
     )
+    got = exchange(part, "lev", bits("lev")[-1])
+    near = local(
+        join_kernel,
+        "join",
+        12,
+        pltpu.VMEM(near.shape, F32),
+        [IN_VMEM] * 4,
+        *map(pinned, (part, got, near, shift)),
+        input_output_aliases={2: 0},
+    )
+    far = after(far, near, kry)
+    got = exchange(near, "tile", 1)
+    part = add(near, got)
+    near = got
+    far = lax.ppermute(
+        far, "tile", [(i, (i + 1 if i % 2 else i - 1) % tiles) for i in range(tiles)]
+    )
+    for bit in bits("tile")[1:-1]:
+        part = add(part, exchange(part, "tile", bit))
+    token = part
+    send, mine = local(
+        functools.partial(below_kernel, bits("lev")[1:]),
+        "below",
+        12,
+        (pltpu.VMEM(mine.shape, F32), pltpu.VMEM(mine.shape, F32)),
+        [IN_VMEM] * (4 + len(above)),
+        *map(pinned, (first, mine, token, kry, *above)),
+    )
+    other = exchange(send, "lev", 1)
+
     fwd, back, cols = local(
         functools.partial(turn_kernel, dims),
         "turn",
@@ -544,11 +543,14 @@
         (
             pltpu.VMEM(far.shape, F32),
             pltpu.VMEM(far.shape, F32),
-            pltpu.VMEM(cols.shape, F32),
+            pltpu.VMEM((height, width), F32),
         ),
         [IN_VMEM] * 5,
         *map(pinned, (seam_turns, near, far, up, down)),
     )
+
+    for bit in bits("tile")[-1:]:
+        part = add(part, exchange(part, "tile", bit))
 
     return pl.pallas_call(
         functools.partial(final_kernel, dims),

time: 29.4 us -> 26.2 us (0.89)
  Pallas kernels: 13.1 us -> 8.15 us
  waiting for transfers between devices: 2.17 us -> 3.53 us
  starting transfers between devices: 13 us -> 14.2 us
  local copies, waits for them, and re-layouts: 0.71 us -> 0.01 us
    pallas_call x13, Pallas kernels: 10.5 us -> 5.52 us  [local(): pl.pallas_call(kernel, out_shape=out_shape, in_specs=in_specs, out_specs=...]
    ppermute x7, waiting for transfers between devices: 2.17 us -> 3.53 us  [exchange(): return lax.ppermute(x, axis, [(i, i ^ bit) for i in range(size)])]
    unnamed x10 -> x2, local copies, waits for them, and re-layouts: 0.71 us -> 0.01 us
    ppermute x1, starting transfers between devices: 2.63 us -> 3.27 us  [per_device(): lax.ppermute(far, 'tile', [(i, (i + 1 if i % 2 else i - 1) % tiles) for i...]
    ppermute x7, starting transfers between devices: 7.8 us -> 8.36 us  [exchange(): return lax.ppermute(x, axis, [(i, i ^ bit) for i in range(size)])]
  transfers between devices with their start and end apart: 9 -> 9, of which waited for: 4 -> 5; matrix products, arithmetic and copies ran while one was open for 0% -> 0% of each run, Pallas kernels for 25% -> 12%
where the time goes in v3:
time: 26.2 us; the launch traced here: 26 us
  starting transfers between devices  14.2 us (54%)
  Pallas kernels  8.15 us (31%)
  waiting for transfers between devices  3.53 us (13%)
    ppermute x7, starting transfers between devices, exchange(): return lax.ppermute(x, axis, [(i, i ^ bit) for i in range(size)])  8.36 us
    pallas_call x13, Pallas kernels, local(): pl.pallas_call(kernel, out_shape=out_shape, in_specs=in_specs, out_specs=...  5.52 us
    ppermute x7, waiting for transfers between devices, exchange(): return lax.ppermute(x, axis, [(i, i ^ bit) for i in range(size)])  3.53 us
    ppermute x1, starting transfers between devices, per_device(): lax.ppermute(far, 'tile', [(i, (i + 1 if i % 2 else i - 1) % tiles) for i...  3.27 us
    pallas_call x1, Pallas kernels, per_device(): pl.pallas_call(functools.partial(final_kernel, dims), out_shape=jax.Shape...  2.62 us
    ppermute x1, starting transfers between devices, shifted(): return lax.ppermute(x, axis, [(i, (i + steps) % size) for i in range(size)])  2.59 us
  transfers between devices with their start and end apart: 9, of which 5 were waited for; matrix products, arithmetic and copies ran while one was open for 0% of the time, Pallas kernels for 12%

profile of v3, /device:TPU:0, one launch (start us, length us, event | category | flops | bytes accessed | tf_op | source)
XLA Modules:
  0.0 26.0 jit_solution(12413072950923551771)
XLA Ops:
  0.0 2.4 %dots.1 = (bf16[4,2,5,256,128]{4,3,2,1,0:T(8,128)(2,1)S(1)}, f32[1032,128]{1,0:T(8,128)S(1)}, f32[1024,128]{1,0:T(8,128)S(1)}, f32[2,5,256,128]{3,2,1,0:T(8,128)S(1)}) custom-call(f32[4,4]{1,0:T(4,128)} %projected.1, bf16[4,2,5,256,128]{4,3,2,1,0:T(8,128)(2,1)} %kry.1, f32[2,5,256,128]{3,2,1,0:T(8,128)} %adj.1), custom_call_target="tpu_custom_call" | custom-call | flops 2000000000 | bytes 7000000 | tf_op jit(solution)/shard_map/dots/pallas_call | solution.py:403
  2.4 0.5 %collective-permute-start = (f32[1032,128]{1,0:T(8,128)S(1)}, f32[1032,128]{1,0:T(8,128)S(1)}, u32[]{:S(2)}, u32[]{:S(2)}) collective-permute-start(f32[1032,128]{1,0:T(8,128)S(1)} %get-tuple-element.22.pack), channel_id=1, source_target_pairs={{0,1},{1,0},{2,3},{3,2},{4,5},{5,4},{6,7},{7,6},{8,9},{9,8},{10,11... | collective-permute-start | bytes 1585160 | tf_op jit(solution)/shard_map/ppermute | solution.py:29
  2.9 1.5 %strips.1 = (bf16[5,2,256,128]{3,2,1,0:T(8,128)(2,1)S(1)}, f32[72,128]{1,0:T(8,128)S(1)}, f32[64,128]{1,0:T(8,128)S(1)}, f32[80,256]{1,0:T(8,128)S(1)}) custom-call(bf16[4,2,5,256,128]{4,3,2,1,0:T(8,128)(2,1)S(1)} %get-tuple-element.23.kry_v.held.kry, bf16[5,2,256,128]{3,2,1,0:T(8,128)(2,1)} %sten.1), custom_call_target="tpu_custom_call" | custom-call | flops 1500000000 | bytes 5250000 | tf_op jit(solution)/shard_map/strips/pallas_call | solution.py:403
  4.4 0.1 collective-permute-done.got
  4.5 2.9 %collective-permute-start.1 = (f32[8,128]{1,0:T(8,128)S(1)}, f32[8,128]{1,0:T(8,128)S(1)}, u32[]{:S(2)}, u32[]{:S(2)}) collective-permute-start(f32[8,128]{1,0:T(8,128)S(1)} %pair.1.token.a), channel_id=1, source_target_pairs={{0,2},{1,3},{2,0},{3,1},{4,6},{5,7},{6,4},{7,5},{8,10},{9,11},{10,... | collective-permute-start | bytes 12296 | tf_op jit(solution)/shard_map/ppermute | solution.py:29
  7.4 0.1 segment.1
  7.4 0.1 collective-permute-start.7
  7.5 1.1 %tables.1 = (bf16[4,2,256,128]{3,2,1,0:T(8,128)(2,1)S(1)}, bf16[256,256]{1,0:T(8,128)(2,1)S(1)}, bf16[10,256,256]{2,1,0:T(8,128)(2,1)S(1)}, f32[2,2,256,128]{3,2,1,0:T(8,128)S(1)}) custom-call(bf16[5,2,256,128]{3,2,1,0:T(8,128)(2,1)S(1)} %get-tuple-element.25.sten, f32[2,2,256,128]{3,2,1,0:T(8,128)} %cw.1, f32[8,128]{1,0:T(8,128)S(1)} %pair.1.token.a), custom_call_target="tpu_custom_call" | custom-call | flops 1500000000 | bytes 5250000 | tf_op jit(solution)/shard_map/tables/pallas_call | solution.py:403
  8.6 0.4 %collective-permute-done.1.b = f32[8,128]{1,0:T(8,128)S(1)} collective-permute-done((f32[8,128]{1,0:T(8,128)S(1)}, f32[8,128]{1,0:T(8,128)S(1)}, u32[]{:S(2)}, u32[]{:S(2)}) %collective-permute-start.1) | collective-permute-done | bytes 4128 | tf_op jit(solution)/shard_map/ppermute | solution.py:29
  9.0 2.0 %collective-permute-start.2 = (f32[72,128]{1,0:T(8,128)S(1)}, f32[72,128]{1,0:T(8,128)S(1)}, u32[]{:S(2)}, u32[]{:S(2)}) collective-permute-start(f32[72,128]{1,0:T(8,128)S(1)} %join.1.a.token), channel_id=1, source_target_pairs={{0,4},{4,0},{8,12},{12,8},{16,20},{20,16},{24,28},{28,24},{1,5},{5... | collective-permute-start | bytes 110600 | tf_op jit(solution)/shard_map/ppermute | solution.py:29
  11.0 2.6 %collective-permute-start.6 = (f32[80,256]{1,0:T(8,128)S(1)}, f32[80,256]{1,0:T(8,128)S(1)}, u32[]{:S(2)}, u32[]{:S(2)}) collective-permute-start(f32[80,256]{1,0:T(8,128)S(1)} %after.3), channel_id=1, source_target_pairs={{0,16},{4,20},{8,24},{12,28},{16,0},{20,4},{24,8},{28,12},{1,17},{... | collective-permute-start | bytes 245768 | tf_op jit(solution)/shard_map/ppermute | solution.py:34
  13.5 0.0 collective-permute-done.2.b.near
  13.6 1.6 %collective-permute-start.3 = (f32[8,128]{1,0:T(8,128)S(1)}, f32[8,128]{1,0:T(8,128)S(1)}, u32[]{:S(2)}, u32[]{:S(2)}) collective-permute-start(f32[8,128]{1,0:T(8,128)S(1)} %add.3.a), channel_id=1, source_target_pairs={{0,8},{4,12},{8,0},{12,4},{16,24},{20,28},{24,16},{28,20},{1,9},{5... | collective-permute-start | bytes 12296 | tf_op jit(solution)/shard_map/ppermute | solution.py:29
  15.1 3.3 %collective-permute-start.5 = (f32[64,128]{1,0:T(8,128)S(1)}, f32[64,128]{1,0:T(8,128)S(1)}, u32[]{:S(2)}, u32[]{:S(2)}) collective-permute-start(f32[64,128]{1,0:T(8,128)S(1)} %after.2), channel_id=1, source_target_pairs={{0,28},{4,8},{8,4},{12,16},{16,12},{20,24},{24,20},{28,0},{1,29},{... | collective-permute-start | bytes 98312 | tf_op jit(solution)/shard_map/ppermute | solution.py:523
  18.4 0.0 collective-permute-done.3.b
  18.4 1.2 %collective-permute-start.4 = (f32[8,128]{1,0:T(8,128)S(1)}, f32[8,128]{1,0:T(8,128)S(1)}, u32[]{:S(2)}, u32[]{:S(2)}) collective-permute-start(f32[8,128]{1,0:T(8,128)S(1)} %add.4.a.token), channel_id=1, source_target_pairs={{0,16},{4,20},{8,24},{12,28},{16,0},{20,4},{24,8},{28,12},{1,17},{... | collective-permute-start | bytes 12296 | tf_op jit(solution)/shard_map/ppermute | solution.py:29
  19.6 1.5 %collective-permute-done.7.refs_0_ = f32[1024,128]{1,0:T(8,128)S(1)} collective-permute-done((f32[1024,128]{1,0:T(8,128)S(1)}, f32[1024,128]{1,0:T(8,128)S(1)}, u32[]{:S(2)}, u32[]{:S(2)}) %collective-permute-start.7) | collective-permute-done | bytes 524320 | tf_op jit(solution)/shard_map/ppermute | solution.py:29
  21.2 0.2 below.1
  21.4 0.0 copy-start
  21.4 0.1 collective-permute-start.8
  21.5 1.5 %collective-permute-done.4.b = f32[8,128]{1,0:T(8,128)S(1)} collective-permute-done((f32[8,128]{1,0:T(8,128)S(1)}, f32[8,128]{1,0:T(8,128)S(1)}, u32[]{:S(2)}, u32[]{:S(2)}) %collective-permute-start.4) | collective-permute-done | bytes 4128 | tf_op jit(solution)/shard_map/ppermute | solution.py:29
  22.9 0.0 collective-permute-done.5.far
  22.9 0.0 collective-permute-done.6.up.down
  22.9 0.0 copy-done
  22.9 0.3 %turn.1 = (f32[64,128]{1,0:T(8,128)S(1)}, f32[64,128]{1,0:T(8,128)S(1)}, f32[256,128]{1,0:T(8,128)S(1)}) custom-call(s32[1,4]{1,0:T(1,128)S(1)} %copy-done, f32[72,128]{1,0:T(8,128)S(1)} %collective-permute-done.2.b.near, f32[64,128]{1,0:T(8,128)S(1)} %collective-permute-done.5.far, f32[80,256]{1,0:T(8,128)S(1)} %collective-permute-done.6.up.down, ...), custom_call_target="tpu_custom_call" | custom-call | flops 1000000000 | bytes 3500000 | tf_op jit(solution)/shard_map/turn/pallas_call | solution.py:403
  23.3 0.1 collective-permute-done.8.other
  23.4 2.6 %final.1 = f32[2,5,256,128]{3,2,1,0:T(8,128)} custom-call(f32[8,128]{1,0:T(8,128)S(1)} %add.5.part, bf16[4,2,5,256,128]{4,3,2,1,0:T(8,128)(2,1)S(1)} %get-tuple-element.23.kry_v.held.kry, f32[2,5,256,128]{3,2,1,0:T(8,128)S(1)} %get-tuple-element.27.adj, bf16[5,2,256,128]{3,2,1,0:T(8,128)(2,1)S(1)} %get-tuple-element.25.sten, ...), custom_call_target="tpu_custom_call" | custom-call | tf_op jit(solution)/shard_map/final/pallas_call | solution.py:555
  (7 shorter events, 0.0 us)
Async XLA Ops:
  2.4 2.1 %collective-permute-start = (f32[1032,128]{1,0:T(8,128)S(1)}, f32[1032,128]{1,0:T(8,128)S(1)}, u32[]{:S(2)}, u32[]{:S(2)}) collective-permute-start(f32[1032,128]{1,0:T(8,128)S(1)} %get-tuple-element.22.pack), channel_id=1, source_target_pairs={{0,1},{1,0},{2,3},{3,2},{4,5},{5,4},{6,7},{7,6},{8,9},{9,8},{10,11... | collective-permute-start | bytes 1585160 | tf_op jit(solution)/shard_map/ppermute | solution.py:29
  4.5 4.5 %collective-permute-start.1 = (f32[8,128]{1,0:T(8,128)S(1)}, f32[8,128]{1,0:T(8,128)S(1)}, u32[]{:S(2)}, u32[]{:S(2)}) collective-permute-start(f32[8,128]{1,0:T(8,128)S(1)} %pair.1.token.a), channel_id=1, source_target_pairs={{0,2},{1,3},{2,0},{3,1},{4,6},{5,7},{6,4},{7,5},{8,10},{9,11},{10,... | collective-permute-start | bytes 12296 | tf_op jit(solution)/shard_map/ppermute | solution.py:29
  7.4 13.8 %collective-permute-start.7 = (f32[1024,128]{1,0:T(8,128)S(1)}, f32[1024,128]{1,0:T(8,128)S(1)}, u32[]{:S(2)}, u32[]{:S(2)}) collective-permute-start(f32[1024,128]{1,0:T(8,128)S(1)} %segment.1), channel_id=1, source_target_pairs={{0,2},{1,3},{2,0},{3,1},{4,6},{5,7},{6,4},{7,5},{8,10},{9,11},{10,... | collective-permute-start | bytes 1572872 | tf_op jit(solution)/shard_map/ppermute | solution.py:29
  9.0 4.6 %collective-permute-start.2 = (f32[72,128]{1,0:T(8,128)S(1)}, f32[72,128]{1,0:T(8,128)S(1)}, u32[]{:S(2)}, u32[]{:S(2)}) collective-permute-start(f32[72,128]{1,0:T(8,128)S(1)} %join.1.a.token), channel_id=1, source_target_pairs={{0,4},{4,0},{8,12},{12,8},{16,20},{20,16},{24,28},{28,24},{1,5},{5... | collective-permute-start | bytes 110600 | tf_op jit(solution)/shard_map/ppermute | solution.py:29
  11.0 12.0 %collective-permute-start.6 = (f32[80,256]{1,0:T(8,128)S(1)}, f32[80,256]{1,0:T(8,128)S(1)}, u32[]{:S(2)}, u32[]{:S(2)}) collective-permute-start(f32[80,256]{1,0:T(8,128)S(1)} %after.3), channel_id=1, source_target_pairs={{0,16},{4,20},{8,24},{12,28},{16,0},{20,4},{24,8},{28,12},{1,17},{... | collective-permute-start | bytes 245768 | tf_op jit(solution)/shard_map/ppermute | solution.py:34
  13.6 4.9 %collective-permute-start.3 = (f32[8,128]{1,0:T(8,128)S(1)}, f32[8,128]{1,0:T(8,128)S(1)}, u32[]{:S(2)}, u32[]{:S(2)}) collective-permute-start(f32[8,128]{1,0:T(8,128)S(1)} %add.3.a), channel_id=1, source_target_pairs={{0,8},{4,12},{8,0},{12,4},{16,24},{20,28},{24,16},{28,20},{1,9},{5... | collective-permute-start | bytes 12296 | tf_op jit(solution)/shard_map/ppermute | solution.py:29
  15.1 7.8 %collective-permute-start.5 = (f32[64,128]{1,0:T(8,128)S(1)}, f32[64,128]{1,0:T(8,128)S(1)}, u32[]{:S(2)}, u32[]{:S(2)}) collective-permute-start(f32[64,128]{1,0:T(8,128)S(1)} %after.2), channel_id=1, source_target_pairs={{0,28},{4,8},{8,4},{12,16},{16,12},{20,24},{24,20},{28,0},{1,29},{... | collective-permute-start | bytes 98312 | tf_op jit(solution)/shard_map/ppermute | solution.py:523
  18.4 4.5 %collective-permute-start.4 = (f32[8,128]{1,0:T(8,128)S(1)}, f32[8,128]{1,0:T(8,128)S(1)}, u32[]{:S(2)}, u32[]{:S(2)}) collective-permute-start(f32[8,128]{1,0:T(8,128)S(1)} %add.4.a.token), channel_id=1, source_target_pairs={{0,16},{4,20},{8,24},{12,28},{16,0},{20,4},{24,8},{28,12},{1,17},{... | collective-permute-start | bytes 12296 | tf_op jit(solution)/shard_map/ppermute | solution.py:29
  21.4 1.6 %copy-start = (s32[1,4]{1,0:T(1,128)S(1)}, s32[1,4]{1,0:T(1,128)}, u32[]{:S(2)}) copy-start(s32[1,4]{1,0:T(1,128)} %turns.1) | copy-start | bytes 52
  21.4 2.0 %collective-permute-start.8 = (f32[1024,128]{1,0:T(8,128)S(1)}, f32[1024,128]{1,0:T(8,128)S(1)}, u32[]{:S(2)}, u32[]{:S(2)}) collective-permute-start(f32[1024,128]{1,0:T(8,128)S(1)} %get-tuple-element.38), channel_id=1, source_target_pairs={{0,1},{1,0},{2,3},{3,2},{4,5},{5,4},{6,7},{7,6},{8,9},{9,8},{10,11... | collective-permute-start | bytes 1572872 | tf_op jit(solution)/shard_map/ppermute | solution.py:29

commit v4 on v3

--- a/solution.py
+++ b/solution.py
@@ -278,56 +278,67 @@
                 times(mix[k], kry[k, l, f, at].astype(F32)) for k in range(vectors)
             )
 
-    def column(c):
-        for i in range(height // step):
-            at = slice(i * step, (i + 1) * step)
-            x = 0.0
-            for k in range(half):
-                here = slice((k * 2 + c) * height + i * step, (k * 2 + c) * height + (i + 1) * step)
-                x = x + (times(mine_mix[k], mine[here]) + times(other_mix[k], other[here]))
-            for l in reversed(range(levels)):
-                q = l * fields + (0 if c == 0 else 3)
-                x = x + comb[q, 8 + i * step : 8 + (i + 1) * step]
-                low[c, l, at] = cw[c, l, at] * x
+    def column(l):
+        for c, f in ((0, 0), (1, 3)):
+            for i in range(height // step):
+                at = slice(i * step, (i + 1) * step)
+                if l == levels - 1:
+                    x = 0.0
+                    for k in range(half):
+                        start = (k * 2 + c) * height + i * step
+                        x = x + (
+                            times(mine_mix[k], mine[start : start + step])
+                            + times(other_mix[k], other[start : start + step])
+                        )
+                else:
+                    x = low[c, at]
+                low[c, at] = x + comb[l * fields + f, 8 + i * step : 8 + (i + 1) * step]
 
     def move(l, f):
         q = l * fields + f
         x = comb[q, 8 : 8 + height]
-        moved[q % 2] = jnp.dot(split(x), shift[...], preferred_element_type=F32) + jnp.dot(
+        moved[f] = jnp.dot(split(x), shift[...], preferred_element_type=F32) + jnp.dot(
             edges[...], spots[q], preferred_element_type=F32
         )
 
-    def stencil(l, f):
-        q = l * fields + f
-        for i in range(height // step):
-            at = slice(i * step, (i + 1) * step)
-            first = 8 + i * step
-            image = (
-                sten[0, l, at].astype(F32) * comb[q, first : first + step]
-                + coefs[0, l, at].astype(F32) * comb[q, first - 1 : first + step - 1]
-                + coefs[1, l, at].astype(F32) * comb[q, first + 1 : first + step + 1]
-                + coefs[2, l, at].astype(F32) * moved[q % 2, at, 0:128]
-                + coefs[3, l, at].astype(F32) * moved[q % 2, at, 128:256]
-            )
-            if f in (1, 4):
-                image = image + low[0 if f == 1 else 1, l, at]
-            out[l, f, at] = adj[l, f, at] + image
-
-    order = [0, 3] + [f for f in range(fields) if f not in (0, 3)]
-    planes = [(l, f) for f in order for l in range(levels)]
-    combine(*planes[0])
     copies = []
-    for n, (l, f) in enumerate(planes):
-        if n + 1 < len(planes):
-            combine(*planes[n + 1])
-        if n == 2 * levels - 1:
-            column(0)
-            column(1)
-        move(l, f)
-        stencil(l, f)
-        copy = pltpu.make_async_copy(out.at[l, f], out_hbm.at[l, f], sem.at[n])
-        copy.start()
-        copies.append(copy)
+
+    def stencil(l):
+        size, block = 32, 64
+        for i in range(height // size):
+            at = slice(i * size, (i + 1) * size)
+            first = 8 + i * size
+            c0 = sten[0, l, at].astype(F32)
+            c1, c2, c3, c4 = (coefs[d, l, at].astype(F32) for d in range(4))
+            for f in range(fields):
+                q = l * fields + f
+                image = (
+                    c0 * comb[q, first : first + size]
+                    + c1 * comb[q, first - 1 : first + size - 1]
+                    + c2 * comb[q, first + 1 : first + size + 1]
+                    + c3 * moved[f, at, 0:128]
+                    + c4 * moved[f, at, 128:256]
+                )
+                if f in (1, 4):
+                    c = 0 if f == 1 else 1
+                    image = image + cw[c, l, at] * low[c, at]
+                out[l, f, at] = adj[l, f, at] + image
+            if (i + 1) * size % block == 0:
+                n = (i + 1) * size // block - 1
+                at = slice(n * block, (n + 1) * block)
+                copy = pltpu.make_async_copy(
+                    out.at[l, :, at], out_hbm.at[l, :, at], sem.at[len(copies)]
+                )
+                copy.start()
+                copies.append(copy)
+
+    for l in reversed(range(levels)):
+        for f in range(fields):
+            combine(l, f)
+        column(l)
+        for f in range(fields):
+            move(l, f)
+        stencil(l)
     for copy in copies:
         copy.wait()
 
@@ -336,11 +347,11 @@
     _, levels, fields, height = dims
     return [
         pltpu.VMEM((levels * fields, height + 16, 128), F32),
-        pltpu.VMEM((2, levels, height, 128), F32),
+        pltpu.VMEM((2, height, 128), F32),
         pltpu.VMEM((height, 256), jnp.bfloat16),
-        pltpu.VMEM((2, height, 256), F32),
+        pltpu.VMEM((fields, height, 256), F32),
         pltpu.VMEM((levels, fields, height, 128), F32),
-        pltpu.SemaphoreType.DMA((levels * fields,)),
+        pltpu.SemaphoreType.DMA((levels * height // 64,)),
     ]
 
 

time: 26.2 us -> 26 us (level)
  no operation moved by 1% of the time
where the time goes in v4:
time: 26 us; the launch traced here: 25.8 us
  starting transfers between devices  14.2 us (55%)
  Pallas kernels  7.98 us (31%)
  waiting for transfers between devices  3.53 us (14%)
    ppermute x7, starting transfers between devices, exchange(): return lax.ppermute(x, axis, [(i, i ^ bit) for i in range(size)])  8.36 us
    pallas_call x13, Pallas kernels, local(): pl.pallas_call(kernel, out_shape=out_shape, in_specs=in_specs, out_specs=...  5.52 us
    ppermute x7, waiting for transfers between devices, exchange(): return lax.ppermute(x, axis, [(i, i ^ bit) for i in range(size)])  3.53 us
    ppermute x1, starting transfers between devices, per_device(): lax.ppermute(far, 'tile', [(i, (i + 1 if i % 2 else i - 1) % tiles) for i...  3.27 us
    ppermute x1, starting transfers between devices, shifted(): return lax.ppermute(x, axis, [(i, (i + steps) % size) for i in range(size)])  2.59 us
    pallas_call x1, Pallas kernels, per_device(): pl.pallas_call(functools.partial(final_kernel, dims), out_shape=jax.Shape...  2.45 us
  transfers between devices with their start and end apart: 9, of which 5 were waited for; matrix products, arithmetic and copies ran while one was open for 0% of the time, Pallas kernels for 12%

profile of v4, /device:TPU:0, one launch (start us, length us, event | category | flops | bytes accessed | tf_op | source)
XLA Modules:
  0.0 25.8 jit_solution(10515947217719310893)
XLA Ops:
  0.0 2.4 %dots.1 = (bf16[4,2,5,256,128]{4,3,2,1,0:T(8,128)(2,1)S(1)}, f32[1032,128]{1,0:T(8,128)S(1)}, f32[1024,128]{1,0:T(8,128)S(1)}, f32[2,5,256,128]{3,2,1,0:T(8,128)S(1)}) custom-call(f32[4,4]{1,0:T(4,128)} %projected.1, bf16[4,2,5,256,128]{4,3,2,1,0:T(8,128)(2,1)} %kry.1, f32[2,5,256,128]{3,2,1,0:T(8,128)} %adj.1), custom_call_target="tpu_custom_call" | custom-call | flops 2000000000 | bytes 7000000 | tf_op jit(solution)/shard_map/dots/pallas_call | solution.py:414
  2.4 0.5 %collective-permute-start = (f32[1032,128]{1,0:T(8,128)S(1)}, f32[1032,128]{1,0:T(8,128)S(1)}, u32[]{:S(2)}, u32[]{:S(2)}) collective-permute-start(f32[1032,128]{1,0:T(8,128)S(1)} %get-tuple-element.22.pack), channel_id=1, source_target_pairs={{0,1},{1,0},{2,3},{3,2},{4,5},{5,4},{6,7},{7,6},{8,9},{9,8},{10,11... | collective-permute-start | bytes 1585160 | tf_op jit(solution)/shard_map/ppermute | solution.py:29
  2.9 1.5 %strips.1 = (bf16[5,2,256,128]{3,2,1,0:T(8,128)(2,1)S(1)}, f32[72,128]{1,0:T(8,128)S(1)}, f32[64,128]{1,0:T(8,128)S(1)}, f32[80,256]{1,0:T(8,128)S(1)}) custom-call(bf16[4,2,5,256,128]{4,3,2,1,0:T(8,128)(2,1)S(1)} %get-tuple-element.23.kry_v.held.kry, bf16[5,2,256,128]{3,2,1,0:T(8,128)(2,1)} %sten.1), custom_call_target="tpu_custom_call" | custom-call | flops 1500000000 | bytes 5250000 | tf_op jit(solution)/shard_map/strips/pallas_call | solution.py:414
  4.4 0.1 collective-permute-done.got
  4.5 2.9 %collective-permute-start.1 = (f32[8,128]{1,0:T(8,128)S(1)}, f32[8,128]{1,0:T(8,128)S(1)}, u32[]{:S(2)}, u32[]{:S(2)}) collective-permute-start(f32[8,128]{1,0:T(8,128)S(1)} %pair.1.token.a), channel_id=1, source_target_pairs={{0,2},{1,3},{2,0},{3,1},{4,6},{5,7},{6,4},{7,5},{8,10},{9,11},{10,... | collective-permute-start | bytes 12296 | tf_op jit(solution)/shard_map/ppermute | solution.py:29
  7.4 0.1 segment.1
  7.4 0.1 collective-permute-start.7
  7.5 1.1 %tables.1 = (bf16[4,2,256,128]{3,2,1,0:T(8,128)(2,1)S(1)}, bf16[256,256]{1,0:T(8,128)(2,1)S(1)}, bf16[10,256,256]{2,1,0:T(8,128)(2,1)S(1)}, f32[2,2,256,128]{3,2,1,0:T(8,128)S(1)}) custom-call(bf16[5,2,256,128]{3,2,1,0:T(8,128)(2,1)S(1)} %get-tuple-element.25.sten, f32[2,2,256,128]{3,2,1,0:T(8,128)} %cw.1, f32[8,128]{1,0:T(8,128)S(1)} %pair.1.token.a), custom_call_target="tpu_custom_call" | custom-call | flops 1500000000 | bytes 5250000 | tf_op jit(solution)/shard_map/tables/pallas_call | solution.py:414
  8.6 0.4 %collective-permute-done.1.b = f32[8,128]{1,0:T(8,128)S(1)} collective-permute-done((f32[8,128]{1,0:T(8,128)S(1)}, f32[8,128]{1,0:T(8,128)S(1)}, u32[]{:S(2)}, u32[]{:S(2)}) %collective-permute-start.1) | collective-permute-done | bytes 4128 | tf_op jit(solution)/shard_map/ppermute | solution.py:29
  9.0 2.0 %collective-permute-start.2 = (f32[72,128]{1,0:T(8,128)S(1)}, f32[72,128]{1,0:T(8,128)S(1)}, u32[]{:S(2)}, u32[]{:S(2)}) collective-permute-start(f32[72,128]{1,0:T(8,128)S(1)} %join.1.a.token), channel_id=1, source_target_pairs={{0,4},{4,0},{8,12},{12,8},{16,20},{20,16},{24,28},{28,24},{1,5},{5... | collective-permute-start | bytes 110600 | tf_op jit(solution)/shard_map/ppermute | solution.py:29
  11.0 2.6 %collective-permute-start.6 = (f32[80,256]{1,0:T(8,128)S(1)}, f32[80,256]{1,0:T(8,128)S(1)}, u32[]{:S(2)}, u32[]{:S(2)}) collective-permute-start(f32[80,256]{1,0:T(8,128)S(1)} %after.3), channel_id=1, source_target_pairs={{0,16},{4,20},{8,24},{12,28},{16,0},{20,4},{24,8},{28,12},{1,17},{... | collective-permute-start | bytes 245768 | tf_op jit(solution)/shard_map/ppermute | solution.py:34
  13.5 0.0 collective-permute-done.2.b.near
  13.6 1.6 %collective-permute-start.3 = (f32[8,128]{1,0:T(8,128)S(1)}, f32[8,128]{1,0:T(8,128)S(1)}, u32[]{:S(2)}, u32[]{:S(2)}) collective-permute-start(f32[8,128]{1,0:T(8,128)S(1)} %add.3.a), channel_id=1, source_target_pairs={{0,8},{4,12},{8,0},{12,4},{16,24},{20,28},{24,16},{28,20},{1,9},{5... | collective-permute-start | bytes 12296 | tf_op jit(solution)/shard_map/ppermute | solution.py:29
  15.1 3.3 %collective-permute-start.5 = (f32[64,128]{1,0:T(8,128)S(1)}, f32[64,128]{1,0:T(8,128)S(1)}, u32[]{:S(2)}, u32[]{:S(2)}) collective-permute-start(f32[64,128]{1,0:T(8,128)S(1)} %after.2), channel_id=1, source_target_pairs={{0,28},{4,8},{8,4},{12,16},{16,12},{20,24},{24,20},{28,0},{1,29},{... | collective-permute-start | bytes 98312 | tf_op jit(solution)/shard_map/ppermute | solution.py:534
  18.4 0.0 collective-permute-done.3.b
  18.4 1.2 %collective-permute-start.4 = (f32[8,128]{1,0:T(8,128)S(1)}, f32[8,128]{1,0:T(8,128)S(1)}, u32[]{:S(2)}, u32[]{:S(2)}) collective-permute-start(f32[8,128]{1,0:T(8,128)S(1)} %add.4.a.token), channel_id=1, source_target_pairs={{0,16},{4,20},{8,24},{12,28},{16,0},{20,4},{24,8},{28,12},{1,17},{... | collective-permute-start | bytes 12296 | tf_op jit(solution)/shard_map/ppermute | solution.py:29
  19.6 1.5 %collective-permute-done.7.refs_0_ = f32[1024,128]{1,0:T(8,128)S(1)} collective-permute-done((f32[1024,128]{1,0:T(8,128)S(1)}, f32[1024,128]{1,0:T(8,128)S(1)}, u32[]{:S(2)}, u32[]{:S(2)}) %collective-permute-start.7) | collective-permute-done | bytes 524320 | tf_op jit(solution)/shard_map/ppermute | solution.py:29
  21.2 0.2 below.1
  21.4 0.0 copy-start
  21.4 0.1 collective-permute-start.8
  21.5 1.5 %collective-permute-done.4.b = f32[8,128]{1,0:T(8,128)S(1)} collective-permute-done((f32[8,128]{1,0:T(8,128)S(1)}, f32[8,128]{1,0:T(8,128)S(1)}, u32[]{:S(2)}, u32[]{:S(2)}) %collective-permute-start.4) | collective-permute-done | bytes 4128 | tf_op jit(solution)/shard_map/ppermute | solution.py:29
  22.9 0.0 collective-permute-done.5.far
  22.9 0.0 collective-permute-done.6.up.down
  22.9 0.0 copy-done
  22.9 0.3 %turn.1 = (f32[64,128]{1,0:T(8,128)S(1)}, f32[64,128]{1,0:T(8,128)S(1)}, f32[256,128]{1,0:T(8,128)S(1)}) custom-call(s32[1,4]{1,0:T(1,128)S(1)} %copy-done, f32[72,128]{1,0:T(8,128)S(1)} %collective-permute-done.2.b.near, f32[64,128]{1,0:T(8,128)S(1)} %collective-permute-done.5.far, f32[80,256]{1,0:T(8,128)S(1)} %collective-permute-done.6.up.down, ...), custom_call_target="tpu_custom_call" | custom-call | flops 1000000000 | bytes 3500000 | tf_op jit(solution)/shard_map/turn/pallas_call | solution.py:414
  23.3 0.1 collective-permute-done.8.other
  23.4 2.5 %final.1 = f32[2,5,256,128]{3,2,1,0:T(8,128)} custom-call(f32[8,128]{1,0:T(8,128)S(1)} %add.5.part, bf16[4,2,5,256,128]{4,3,2,1,0:T(8,128)(2,1)S(1)} %get-tuple-element.23.kry_v.held.kry, f32[2,5,256,128]{3,2,1,0:T(8,128)S(1)} %get-tuple-element.27.adj, bf16[5,2,256,128]{3,2,1,0:T(8,128)(2,1)S(1)} %get-tuple-element.25.sten, ...), custom_call_target="tpu_custom_call" | custom-call | tf_op jit(solution)/shard_map/final/pallas_call | solution.py:566
  (7 shorter events, 0.0 us)
Async XLA Ops:
  2.4 2.1 %collective-permute-start = (f32[1032,128]{1,0:T(8,128)S(1)}, f32[1032,128]{1,0:T(8,128)S(1)}, u32[]{:S(2)}, u32[]{:S(2)}) collective-permute-start(f32[1032,128]{1,0:T(8,128)S(1)} %get-tuple-element.22.pack), channel_id=1, source_target_pairs={{0,1},{1,0},{2,3},{3,2},{4,5},{5,4},{6,7},{7,6},{8,9},{9,8},{10,11... | collective-permute-start | bytes 1585160 | tf_op jit(solution)/shard_map/ppermute | solution.py:29
  4.5 4.5 %collective-permute-start.1 = (f32[8,128]{1,0:T(8,128)S(1)}, f32[8,128]{1,0:T(8,128)S(1)}, u32[]{:S(2)}, u32[]{:S(2)}) collective-permute-start(f32[8,128]{1,0:T(8,128)S(1)} %pair.1.token.a), channel_id=1, source_target_pairs={{0,2},{1,3},{2,0},{3,1},{4,6},{5,7},{6,4},{7,5},{8,10},{9,11},{10,... | collective-permute-start | bytes 12296 | tf_op jit(solution)/shard_map/ppermute | solution.py:29
  7.4 13.8 %collective-permute-start.7 = (f32[1024,128]{1,0:T(8,128)S(1)}, f32[1024,128]{1,0:T(8,128)S(1)}, u32[]{:S(2)}, u32[]{:S(2)}) collective-permute-start(f32[1024,128]{1,0:T(8,128)S(1)} %segment.1), channel_id=1, source_target_pairs={{0,2},{1,3},{2,0},{3,1},{4,6},{5,7},{6,4},{7,5},{8,10},{9,11},{10,... | collective-permute-start | bytes 1572872 | tf_op jit(solution)/shard_map/ppermute | solution.py:29
  9.0 4.6 %collective-permute-start.2 = (f32[72,128]{1,0:T(8,128)S(1)}, f32[72,128]{1,0:T(8,128)S(1)}, u32[]{:S(2)}, u32[]{:S(2)}) collective-permute-start(f32[72,128]{1,0:T(8,128)S(1)} %join.1.a.token), channel_id=1, source_target_pairs={{0,4},{4,0},{8,12},{12,8},{16,20},{20,16},{24,28},{28,24},{1,5},{5... | collective-permute-start | bytes 110600 | tf_op jit(solution)/shard_map/ppermute | solution.py:29
  11.0 12.0 %collective-permute-start.6 = (f32[80,256]{1,0:T(8,128)S(1)}, f32[80,256]{1,0:T(8,128)S(1)}, u32[]{:S(2)}, u32[]{:S(2)}) collective-permute-start(f32[80,256]{1,0:T(8,128)S(1)} %after.3), channel_id=1, source_target_pairs={{0,16},{4,20},{8,24},{12,28},{16,0},{20,4},{24,8},{28,12},{1,17},{... | collective-permute-start | bytes 245768 | tf_op jit(solution)/shard_map/ppermute | solution.py:34
  13.6 4.9 %collective-permute-start.3 = (f32[8,128]{1,0:T(8,128)S(1)}, f32[8,128]{1,0:T(8,128)S(1)}, u32[]{:S(2)}, u32[]{:S(2)}) collective-permute-start(f32[8,128]{1,0:T(8,128)S(1)} %add.3.a), channel_id=1, source_target_pairs={{0,8},{4,12},{8,0},{12,4},{16,24},{20,28},{24,16},{28,20},{1,9},{5... | collective-permute-start | bytes 12296 | tf_op jit(solution)/shard_map/ppermute | solution.py:29
  15.1 7.8 %collective-permute-start.5 = (f32[64,128]{1,0:T(8,128)S(1)}, f32[64,128]{1,0:T(8,128)S(1)}, u32[]{:S(2)}, u32[]{:S(2)}) collective-permute-start(f32[64,128]{1,0:T(8,128)S(1)} %after.2), channel_id=1, source_target_pairs={{0,28},{4,8},{8,4},{12,16},{16,12},{20,24},{24,20},{28,0},{1,29},{... | collective-permute-start | bytes 98312 | tf_op jit(solution)/shard_map/ppermute | solution.py:534
  18.4 4.5 %collective-permute-start.4 = (f32[8,128]{1,0:T(8,128)S(1)}, f32[8,128]{1,0:T(8,128)S(1)}, u32[]{:S(2)}, u32[]{:S(2)}) collective-permute-start(f32[8,128]{1,0:T(8,128)S(1)} %add.4.a.token), channel_id=1, source_target_pairs={{0,16},{4,20},{8,24},{12,28},{16,0},{20,4},{24,8},{28,12},{1,17},{... | collective-permute-start | bytes 12296 | tf_op jit(solution)/shard_map/ppermute | solution.py:29
  21.4 1.6 %copy-start = (s32[1,4]{1,0:T(1,128)S(1)}, s32[1,4]{1,0:T(1,128)}, u32[]{:S(2)}) copy-start(s32[1,4]{1,0:T(1,128)} %turns.1) | copy-start | bytes 52
  21.4 2.0 %collective-permute-start.8 = (f32[1024,128]{1,0:T(8,128)S(1)}, f32[1024,128]{1,0:T(8,128)S(1)}, u32[]{:S(2)}, u32[]{:S(2)}) collective-permute-start(f32[1024,128]{1,0:T(8,128)S(1)} %get-tuple-element.38), channel_id=1, source_target_pairs={{0,1},{1,0},{2,3},{3,2},{4,5},{5,4},{6,7},{7,6},{8,9},{9,8},{10,11... | collective-permute-start | bytes 1572872 | tf_op jit(solution)/shard_map/ppermute | solution.py:29

commit v5 on v4

--- a/solution.py
+++ b/solution.py
@@ -383,7 +383,7 @@
     return local(
         keep_kernel,
         "after",
-        12,
+        6,
         pltpu.VMEM(x.shape, F32),
         [IN_VMEM] * 3,
         *map(pinned, (x, token, held)),
@@ -427,7 +427,7 @@
 
 def add(a, b, *held):
     return local(
-        add_kernel, "add", 12, pltpu.VMEM((8, 128), F32), [IN_VMEM] * (2 + len(held)),
+        add_kernel, "add", 6, pltpu.VMEM((8, 128), F32), [IN_VMEM] * (2 + len(held)),
         *map(pinned, (a, b, *held)),
     )
 
@@ -485,7 +485,7 @@
     segment = local(
         segment_kernel,
         "segment",
-        12,
+        6,
         pltpu.VMEM(mine.shape, F32),
         [IN_VMEM] * 4,
         *map(pinned, (first, mine, part, kry)),
@@ -521,7 +521,7 @@
     near = local(
         join_kernel,
         "join",
-        12,
+        6,
         pltpu.VMEM(near.shape, F32),
         [IN_VMEM] * 4,
         *map(pinned, (part, got, near, shift)),
@@ -540,7 +540,7 @@
     send, mine = local(
         functools.partial(below_kernel, bits("lev")[1:]),
         "below",
-        12,
+        6,
         (pltpu.VMEM(mine.shape, F32), pltpu.VMEM(mine.shape, F32)),
         [IN_VMEM] * (4 + len(above)),
         *map(pinned, (first, mine, token, kry, *above)),

time: 26 us -> 26 us (level)
  no operation moved by 1% of the time
where the time goes in v5:
time: 26 us; the launch traced here: 25.8 us
  starting transfers between devices  14.2 us (55%)
  Pallas kernels  7.98 us (31%)
  waiting for transfers between devices  3.53 us (14%)
    ppermute x7, starting transfers between devices, exchange(): return lax.ppermute(x, axis, [(i, i ^ bit) for i in range(size)])  8.36 us
    pallas_call x13, Pallas kernels, local(): pl.pallas_call(kernel, out_shape=out_shape, in_specs=in_specs, out_specs=...  5.52 us
    ppermute x7, waiting for transfers between devices, exchange(): return lax.ppermute(x, axis, [(i, i ^ bit) for i in range(size)])  3.53 us
    ppermute x1, starting transfers between devices, per_device(): lax.ppermute(far, 'tile', [(i, (i + 1 if i % 2 else i - 1) % tiles) for i...  3.27 us
    ppermute x1, starting transfers between devices, shifted(): return lax.ppermute(x, axis, [(i, (i + steps) % size) for i in range(size)])  2.59 us
    pallas_call x1, Pallas kernels, per_device(): pl.pallas_call(functools.partial(final_kernel, dims), out_shape=jax.Shape...  2.45 us
  transfers between devices with their start and end apart: 9, of which 5 were waited for; matrix products, arithmetic and copies ran while one was open for 0% of the time, Pallas kernels for 12%

profile of v5, /device:TPU:0, one launch (start us, length us, event | category | flops | bytes accessed | tf_op | source)
XLA Modules:
  0.0 25.8 jit_solution(10515947217719310893)
XLA Ops:
  0.0 2.4 %dots.1 = (bf16[4,2,5,256,128]{4,3,2,1,0:T(8,128)(2,1)S(1)}, f32[1032,128]{1,0:T(8,128)S(1)}, f32[1024,128]{1,0:T(8,128)S(1)}, f32[2,5,256,128]{3,2,1,0:T(8,128)S(1)}) custom-call(f32[4,4]{1,0:T(4,128)} %projected.1, bf16[4,2,5,256,128]{4,3,2,1,0:T(8,128)(2,1)} %kry.1, f32[2,5,256,128]{3,2,1,0:T(8,128)} %adj.1), custom_call_target="tpu_custom_call" | custom-call | flops 2000000000 | bytes 7000000 | tf_op jit(solution)/shard_map/dots/pallas_call | solution.py:414
  2.4 0.5 %collective-permute-start = (f32[1032,128]{1,0:T(8,128)S(1)}, f32[1032,128]{1,0:T(8,128)S(1)}, u32[]{:S(2)}, u32[]{:S(2)}) collective-permute-start(f32[1032,128]{1,0:T(8,128)S(1)} %get-tuple-element.22.pack), channel_id=1, source_target_pairs={{0,1},{1,0},{2,3},{3,2},{4,5},{5,4},{6,7},{7,6},{8,9},{9,8},{10,11... | collective-permute-start | bytes 1585160 | tf_op jit(solution)/shard_map/ppermute | solution.py:29
  2.9 1.5 %strips.1 = (bf16[5,2,256,128]{3,2,1,0:T(8,128)(2,1)S(1)}, f32[72,128]{1,0:T(8,128)S(1)}, f32[64,128]{1,0:T(8,128)S(1)}, f32[80,256]{1,0:T(8,128)S(1)}) custom-call(bf16[4,2,5,256,128]{4,3,2,1,0:T(8,128)(2,1)S(1)} %get-tuple-element.23.kry_v.held.kry, bf16[5,2,256,128]{3,2,1,0:T(8,128)(2,1)} %sten.1), custom_call_target="tpu_custom_call" | custom-call | flops 1500000000 | bytes 5250000 | tf_op jit(solution)/shard_map/strips/pallas_call | solution.py:414
  4.4 0.1 collective-permute-done.got
  4.5 2.9 %collective-permute-start.1 = (f32[8,128]{1,0:T(8,128)S(1)}, f32[8,128]{1,0:T(8,128)S(1)}, u32[]{:S(2)}, u32[]{:S(2)}) collective-permute-start(f32[8,128]{1,0:T(8,128)S(1)} %pair.1.token.a), channel_id=1, source_target_pairs={{0,2},{1,3},{2,0},{3,1},{4,6},{5,7},{6,4},{7,5},{8,10},{9,11},{10,... | collective-permute-start | bytes 12296 | tf_op jit(solution)/shard_map/ppermute | solution.py:29
  7.4 0.1 segment.1
  7.4 0.1 collective-permute-start.7
  7.5 1.1 %tables.1 = (bf16[4,2,256,128]{3,2,1,0:T(8,128)(2,1)S(1)}, bf16[256,256]{1,0:T(8,128)(2,1)S(1)}, bf16[10,256,256]{2,1,0:T(8,128)(2,1)S(1)}, f32[2,2,256,128]{3,2,1,0:T(8,128)S(1)}) custom-call(bf16[5,2,256,128]{3,2,1,0:T(8,128)(2,1)S(1)} %get-tuple-element.25.sten, f32[2,2,256,128]{3,2,1,0:T(8,128)} %cw.1, f32[8,128]{1,0:T(8,128)S(1)} %pair.1.token.a), custom_call_target="tpu_custom_call" | custom-call | flops 1500000000 | bytes 5250000 | tf_op jit(solution)/shard_map/tables/pallas_call | solution.py:414
  8.6 0.4 %collective-permute-done.1.b = f32[8,128]{1,0:T(8,128)S(1)} collective-permute-done((f32[8,128]{1,0:T(8,128)S(1)}, f32[8,128]{1,0:T(8,128)S(1)}, u32[]{:S(2)}, u32[]{:S(2)}) %collective-permute-start.1) | collective-permute-done | bytes 4128 | tf_op jit(solution)/shard_map/ppermute | solution.py:29
  9.0 2.0 %collective-permute-start.2 = (f32[72,128]{1,0:T(8,128)S(1)}, f32[72,128]{1,0:T(8,128)S(1)}, u32[]{:S(2)}, u32[]{:S(2)}) collective-permute-start(f32[72,128]{1,0:T(8,128)S(1)} %join.1.a.token), channel_id=1, source_target_pairs={{0,4},{4,0},{8,12},{12,8},{16,20},{20,16},{24,28},{28,24},{1,5},{5... | collective-permute-start | bytes 110600 | tf_op jit(solution)/shard_map/ppermute | solution.py:29
  11.0 2.6 %collective-permute-start.6 = (f32[80,256]{1,0:T(8,128)S(1)}, f32[80,256]{1,0:T(8,128)S(1)}, u32[]{:S(2)}, u32[]{:S(2)}) collective-permute-start(f32[80,256]{1,0:T(8,128)S(1)} %after.3), channel_id=1, source_target_pairs={{0,16},{4,20},{8,24},{12,28},{16,0},{20,4},{24,8},{28,12},{1,17},{... | collective-permute-start | bytes 245768 | tf_op jit(solution)/shard_map/ppermute | solution.py:34
  13.5 0.0 collective-permute-done.2.b.near
  13.6 1.6 %collective-permute-start.3 = (f32[8,128]{1,0:T(8,128)S(1)}, f32[8,128]{1,0:T(8,128)S(1)}, u32[]{:S(2)}, u32[]{:S(2)}) collective-permute-start(f32[8,128]{1,0:T(8,128)S(1)} %add.3.a), channel_id=1, source_target_pairs={{0,8},{4,12},{8,0},{12,4},{16,24},{20,28},{24,16},{28,20},{1,9},{5... | collective-permute-start | bytes 12296 | tf_op jit(solution)/shard_map/ppermute | solution.py:29
  15.1 3.3 %collective-permute-start.5 = (f32[64,128]{1,0:T(8,128)S(1)}, f32[64,128]{1,0:T(8,128)S(1)}, u32[]{:S(2)}, u32[]{:S(2)}) collective-permute-start(f32[64,128]{1,0:T(8,128)S(1)} %after.2), channel_id=1, source_target_pairs={{0,28},{4,8},{8,4},{12,16},{16,12},{20,24},{24,20},{28,0},{1,29},{... | collective-permute-start | bytes 98312 | tf_op jit(solution)/shard_map/ppermute | solution.py:534
  18.4 0.0 collective-permute-done.3.b
  18.4 1.2 %collective-permute-start.4 = (f32[8,128]{1,0:T(8,128)S(1)}, f32[8,128]{1,0:T(8,128)S(1)}, u32[]{:S(2)}, u32[]{:S(2)}) collective-permute-start(f32[8,128]{1,0:T(8,128)S(1)} %add.4.a.token), channel_id=1, source_target_pairs={{0,16},{4,20},{8,24},{12,28},{16,0},{20,4},{24,8},{28,12},{1,17},{... | collective-permute-start | bytes 12296 | tf_op jit(solution)/shard_map/ppermute | solution.py:29
  19.6 1.5 %collective-permute-done.7.refs_0_ = f32[1024,128]{1,0:T(8,128)S(1)} collective-permute-done((f32[1024,128]{1,0:T(8,128)S(1)}, f32[1024,128]{1,0:T(8,128)S(1)}, u32[]{:S(2)}, u32[]{:S(2)}) %collective-permute-start.7) | collective-permute-done | bytes 524320 | tf_op jit(solution)/shard_map/ppermute | solution.py:29
  21.2 0.2 below.1
  21.4 0.0 copy-start
  21.4 0.1 collective-permute-start.8
  21.5 1.5 %collective-permute-done.4.b = f32[8,128]{1,0:T(8,128)S(1)} collective-permute-done((f32[8,128]{1,0:T(8,128)S(1)}, f32[8,128]{1,0:T(8,128)S(1)}, u32[]{:S(2)}, u32[]{:S(2)}) %collective-permute-start.4) | collective-permute-done | bytes 4128 | tf_op jit(solution)/shard_map/ppermute | solution.py:29
  22.9 0.0 collective-permute-done.5.far
  22.9 0.0 collective-permute-done.6.up.down
  22.9 0.0 copy-done
  22.9 0.3 %turn.1 = (f32[64,128]{1,0:T(8,128)S(1)}, f32[64,128]{1,0:T(8,128)S(1)}, f32[256,128]{1,0:T(8,128)S(1)}) custom-call(s32[1,4]{1,0:T(1,128)S(1)} %copy-done, f32[72,128]{1,0:T(8,128)S(1)} %collective-permute-done.2.b.near, f32[64,128]{1,0:T(8,128)S(1)} %collective-permute-done.5.far, f32[80,256]{1,0:T(8,128)S(1)} %collective-permute-done.6.up.down, ...), custom_call_target="tpu_custom_call" | custom-call | flops 1000000000 | bytes 3500000 | tf_op jit(solution)/shard_map/turn/pallas_call | solution.py:414
  23.3 0.1 collective-permute-done.8.other
  23.4 2.5 %final.1 = f32[2,5,256,128]{3,2,1,0:T(8,128)} custom-call(f32[8,128]{1,0:T(8,128)S(1)} %add.5.part, bf16[4,2,5,256,128]{4,3,2,1,0:T(8,128)(2,1)S(1)} %get-tuple-element.23.kry_v.held.kry, f32[2,5,256,128]{3,2,1,0:T(8,128)S(1)} %get-tuple-element.27.adj, bf16[5,2,256,128]{3,2,1,0:T(8,128)(2,1)S(1)} %get-tuple-element.25.sten, ...), custom_call_target="tpu_custom_call" | custom-call | tf_op jit(solution)/shard_map/final/pallas_call | solution.py:566
  (7 shorter events, 0.0 us)
Async XLA Ops:
  2.4 2.1 %collective-permute-start = (f32[1032,128]{1,0:T(8,128)S(1)}, f32[1032,128]{1,0:T(8,128)S(1)}, u32[]{:S(2)}, u32[]{:S(2)}) collective-permute-start(f32[1032,128]{1,0:T(8,128)S(1)} %get-tuple-element.22.pack), channel_id=1, source_target_pairs={{0,1},{1,0},{2,3},{3,2},{4,5},{5,4},{6,7},{7,6},{8,9},{9,8},{10,11... | collective-permute-start | bytes 1585160 | tf_op jit(solution)/shard_map/ppermute | solution.py:29
  4.5 4.5 %collective-permute-start.1 = (f32[8,128]{1,0:T(8,128)S(1)}, f32[8,128]{1,0:T(8,128)S(1)}, u32[]{:S(2)}, u32[]{:S(2)}) collective-permute-start(f32[8,128]{1,0:T(8,128)S(1)} %pair.1.token.a), channel_id=1, source_target_pairs={{0,2},{1,3},{2,0},{3,1},{4,6},{5,7},{6,4},{7,5},{8,10},{9,11},{10,... | collective-permute-start | bytes 12296 | tf_op jit(solution)/shard_map/ppermute | solution.py:29
  7.4 13.8 %collective-permute-start.7 = (f32[1024,128]{1,0:T(8,128)S(1)}, f32[1024,128]{1,0:T(8,128)S(1)}, u32[]{:S(2)}, u32[]{:S(2)}) collective-permute-start(f32[1024,128]{1,0:T(8,128)S(1)} %segment.1), channel_id=1, source_target_pairs={{0,2},{1,3},{2,0},{3,1},{4,6},{5,7},{6,4},{7,5},{8,10},{9,11},{10,... | collective-permute-start | bytes 1572872 | tf_op jit(solution)/shard_map/ppermute | solution.py:29
  9.0 4.6 %collective-permute-start.2 = (f32[72,128]{1,0:T(8,128)S(1)}, f32[72,128]{1,0:T(8,128)S(1)}, u32[]{:S(2)}, u32[]{:S(2)}) collective-permute-start(f32[72,128]{1,0:T(8,128)S(1)} %join.1.a.token), channel_id=1, source_target_pairs={{0,4},{4,0},{8,12},{12,8},{16,20},{20,16},{24,28},{28,24},{1,5},{5... | collective-permute-start | bytes 110600 | tf_op jit(solution)/shard_map/ppermute | solution.py:29
  11.0 12.0 %collective-permute-start.6 = (f32[80,256]{1,0:T(8,128)S(1)}, f32[80,256]{1,0:T(8,128)S(1)}, u32[]{:S(2)}, u32[]{:S(2)}) collective-permute-start(f32[80,256]{1,0:T(8,128)S(1)} %after.3), channel_id=1, source_target_pairs={{0,16},{4,20},{8,24},{12,28},{16,0},{20,4},{24,8},{28,12},{1,17},{... | collective-permute-start | bytes 245768 | tf_op jit(solution)/shard_map/ppermute | solution.py:34
  13.6 4.9 %collective-permute-start.3 = (f32[8,128]{1,0:T(8,128)S(1)}, f32[8,128]{1,0:T(8,128)S(1)}, u32[]{:S(2)}, u32[]{:S(2)}) collective-permute-start(f32[8,128]{1,0:T(8,128)S(1)} %add.3.a), channel_id=1, source_target_pairs={{0,8},{4,12},{8,0},{12,4},{16,24},{20,28},{24,16},{28,20},{1,9},{5... | collective-permute-start | bytes 12296 | tf_op jit(solution)/shard_map/ppermute | solution.py:29
  15.1 7.8 %collective-permute-start.5 = (f32[64,128]{1,0:T(8,128)S(1)}, f32[64,128]{1,0:T(8,128)S(1)}, u32[]{:S(2)}, u32[]{:S(2)}) collective-permute-start(f32[64,128]{1,0:T(8,128)S(1)} %after.2), channel_id=1, source_target_pairs={{0,28},{4,8},{8,4},{12,16},{16,12},{20,24},{24,20},{28,0},{1,29},{... | collective-permute-start | bytes 98312 | tf_op jit(solution)/shard_map/ppermute | solution.py:534
  18.4 4.5 %collective-permute-start.4 = (f32[8,128]{1,0:T(8,128)S(1)}, f32[8,128]{1,0:T(8,128)S(1)}, u32[]{:S(2)}, u32[]{:S(2)}) collective-permute-start(f32[8,128]{1,0:T(8,128)S(1)} %add.4.a.token), channel_id=1, source_target_pairs={{0,16},{4,20},{8,24},{12,28},{16,0},{20,4},{24,8},{28,12},{1,17},{... | collective-permute-start | bytes 12296 | tf_op jit(solution)/shard_map/ppermute | solution.py:29
  21.4 1.6 %copy-start = (s32[1,4]{1,0:T(1,128)S(1)}, s32[1,4]{1,0:T(1,128)}, u32[]{:S(2)}) copy-start(s32[1,4]{1,0:T(1,128)} %turns.1) | copy-start | bytes 52
  21.4 2.0 %collective-permute-start.8 = (f32[1024,128]{1,0:T(8,128)S(1)}, f32[1024,128]{1,0:T(8,128)S(1)}, u32[]{:S(2)}, u32[]{:S(2)}) collective-permute-start(f32[1024,128]{1,0:T(8,128)S(1)} %get-tuple-element.38), channel_id=1, source_target_pairs={{0,1},{1,0},{2,3},{3,2},{4,5},{5,4},{6,7},{7,6},{8,9},{9,8},{10,11... | collective-permute-start | bytes 1572872 | tf_op jit(solution)/shard_map/ppermute | solution.py:29
